TPU v7x, 128 devices: a whole 4x4x4 slice. The times are simulated.
128 devices in a mesh: ctx: 16 (over x, z), ch: 8 (over y, core).
Axes of the slice: x: 4, y: 4, z: 4, core: 2. Of those that a mesh axis runs over, the one named last changes fastest.
Arguments:
- conv_input: bfloat16 [8192, 8192], P('ctx', 'ch'), may hold values from -6 to 6
- out_gate: bfloat16 [8192, 8192], P('ctx', 'ch'), may hold values from -6 to 6
- grad_out: bfloat16 [8192, 8192], P('ctx', 'ch'), may hold values from -6 to 6
- pole_rate: float32 [16, 8192], P(None, 'ch'), may hold values from 0 to 1, as said below
- residue: float32 [16, 8192], P(None, 'ch'), may hold values from -1 to 1
- skip_gain: float32 [8192], P('ch'), may hold values from -3 to 3
Outputs:
- input_grad: bfloat16 [8192, 8192], P('ctx', 'ch')
- gate_grad: bfloat16 [8192, 8192], P('ctx', 'ch')
- residue_grad: float32 [16, 8192], P(None, 'ch')
- lograte_grad: float32 [16, 8192], P(None, 'ch')
- skip_grad: float32 [8192], P('ch')
Inputs may be any that keep to these rules, and one draw needn't show every extreme that they name: Positive decay rates; for every pole, exp(-pole_rate) lies in (0, 1).
All inputs are finite; a program needn't handle non-finite values.
Results may differ from a plain program's by a relative error of at most 0.0015.
Values sent between devices are 32-bit elements; how exact they have to be, the bound alone decides.
No kernel may reach another device: no remote copies, remote signals or barrier semaphores. Data moves between devices by JAX's collectives and lax.ppermute only.
A program may use at most 320 MiB of HBM per device.

v0:
```python
import functools
import math

import jax
import jax.numpy as jnp
from jax import lax
from jax.experimental import pallas as pl
from jax.experimental.pallas import tpu as pltpu
from jax.sharding import PartitionSpec as P

CHANNELS = 8192
MODES = 16
LANES = 128
SEGS = 8
SUB = 8
F32 = jnp.float32
PITCH = 72
VMEM_LIMIT = 24 * 1024 * 1024


def rows_of(ref, start, count, stride):
    return ref[pl.ds(start, count, stride=stride), :]


def spread(values):
    return jnp.broadcast_to(values, (SEGS, LANES))


def columns(group):
    return pl.ds(pl.multiple_of(group * LANES, LANES), LANES)


def fetch(hbm, buf, sem, group):
    return pltpu.make_async_copy(hbm.at[:, columns(group)], buf.at[group], sem.at[group])


def order(natural, ordered, values, seg_len):
    for s in range(SEGS):
        natural[pl.ds(s * PITCH, seg_len), :] = values[s * seg_len : (s + 1) * seg_len]
    for q in range(seg_len):
        ordered[q] = rows_of(natural, q, SEGS, PITCH)


def span_kernel(
    x_hbm, o_hbm, g_hbm, rate_hbm, res_hbm, gain_hbm,
    hl_ref, al_ref, hs_ref, as_ref, xq_ref, sq_ref, lam_ref, mu_ref, near_ref, rows_ref, pay_ref,
    x_buf, o_buf, g_buf, rate_buf, res_buf, gain_buf,
    natural, second, rl_t, ends,
    x_sem, o_sem, g_sem, small_sem,
):
    groups, tokens, _ = x_buf.shape
    seg_len = tokens // SEGS
    chunks = seg_len // SUB
    small = [
        pltpu.make_async_copy(hbm, buf, small_sem.at[n])
        for n, (hbm, buf) in enumerate(
            ((rate_hbm, rate_buf), (res_hbm, res_buf), (gain_hbm, gain_buf))
        )
    ]
    for copy in small:
        copy.start()
    for group in range(groups):
        fetch(x_hbm, x_buf, x_sem, group).start()
        fetch(o_hbm, o_buf, o_sem, group).start()
        fetch(g_hbm, g_buf, g_sem, group).start()
    for copy in small:
        copy.wait()
    zero = jnp.zeros((SEGS, LANES), F32)

    def group_step(group, carry):
        cols = columns(group)
        rate = rate_buf[:, cols]
        residue = res_buf[:, cols]
        lam = jnp.exp(-rate)
        mu_rows = jnp.exp(rate * (-float(SUB)))
        big = jnp.exp(rate * (-float(seg_len)))
        rl_rows = residue * lam
        for m in range(MODES):
            lam_ref[group, m] = spread(lam[m : m + 1, :])
            mu_ref[group, m] = spread(mu_rows[m : m + 1, :])
            rl_t[m] = spread(rl_rows[m : m + 1, :])
        rows_ref[0, group] = big
        rows_ref[1, group] = rl_rows
        rows_ref[2, group] = -(rate * residue)
        term = residue
        for d in range(SUB):
            row = jnp.sum(term, axis=0, keepdims=True)
            if d == 0:
                row = row + gain_buf[:, cols]
            near_ref[group, d] = spread(row)
            term = term * lam

        xq = xq_ref.at[group]
        sq = sq_ref.at[group]
        fetch(x_hbm, x_buf, x_sem, group).wait()
        fetch(o_hbm, o_buf, o_sem, group).wait()
        fetch(g_hbm, g_buf, g_sem, group).wait()
        source = x_buf[group].astype(F32)
        signal = g_buf[group].astype(F32) * o_buf[group].astype(F32)
        skip_row = jnp.sum(source * signal, axis=0, keepdims=True)
        order(natural, xq, source, seg_len)
        order(second, sq, signal, seg_len)

        def lag_step(k, acc):
            xs = [xq[k * SUB + j] for j in range(SUB)]
            ss = [sq[k * SUB + j] for j in range(SUB)]
            out = []
            for d in range(SUB):
                total = acc[d]
                for i in range(d, SUB):
                    total = total + ss[i] * xs[i - d]
                out.append(total)
            return tuple(out)

        lagged = lax.fori_loop(0, chunks, lag_step, (zero,) * SUB)
        lag_rows = [jnp.sum(v, axis=0, keepdims=True) for v in lagged]
        res_near = jnp.broadcast_to(lag_rows[0], lam.shape)
        log_near = jnp.zeros_like(lam)
        power = lam
        for d in range(1, SUB):
            term = power * lag_rows[d]
            res_near = res_near + term
            log_near = log_near + float(d) * term
            power = power * lam

        def mode_step(m, carry):
            p1 = lam_ref[group, m]
            mu = mu_ref[group, m]
            rl = rl_t[m]
            p2 = p1 * p1
            p3 = p2 * p1
            p4 = p2 * p2
            pw = [None, p1, p2, p3, p4, p4 * p1, p3 * p3, p4 * p3]
            a_parts = [None] * chunks
            b_parts = [None] * chunks
            for k in reversed(range(chunks)):
                a = sq[k * SUB + SUB - 1] * pw[SUB - 1]
                b = a
                for i in reversed(range(1, SUB - 1)):
                    a = a + sq[k * SUB + i] * pw[i]
                    b = b + a
                a = a + sq[k * SUB]
                a_parts[k] = a
                b_parts[k] = b
                if k == chunks - 1:
                    al_ref[group, k, m] = zero
                    a_run = a
                    b_run = b
                else:
                    al_ref[group, k, m] = rl * a_run
                    b_run = b + mu * (b_run + float(SUB) * a_run)
                    a_run = a + mu * a_run
            for k in range(chunks):
                h = xq[k * SUB] * pw[SUB - 1]
                p = h
                for j in range(1, SUB - 1):
                    h = h + xq[k * SUB + j] * pw[SUB - 1 - j]
                    p = p + h
                h = h + xq[k * SUB + SUB - 1]
                if k == 0:
                    hl_ref[group, k, m] = zero
                    h_run = h
                    p_run = p
                    continue
                hl_ref[group, k, m] = rl * h_run
                res_new = h_run * a_parts[k]
                log_new = p_run * a_parts[k] + h_run * b_parts[k]
                res_x = res_new if k == 1 else res_x + res_new
                log_x = log_new if k == 1 else log_x + log_new
                p_run = p + mu * (p_run + float(SUB) * h_run)
                h_run = h + mu * h_run
            for n, value in enumerate((h_run, p_run, a_run, b_run, res_x, log_x)):
                ends[n, pl.ds(pl.multiple_of(m * SEGS, SEGS), SEGS), :] = value
            return carry

        lax.fori_loop(0, MODES, mode_step, 0)

        def end(n, s):
            return ends[n, pl.ds(s, MODES, stride=SEGS), :]

        span = float(seg_len)
        nothing = jnp.zeros_like(lam)
        h, p, res_x, log_x = nothing, nothing, nothing, nothing
        for s in range(SEGS):
            hs_ref[group, s] = rl_rows * h
            a_s, b_s = end(2, s), end(3, s)
            res_x = res_x + end(4, s) + h * a_s
            log_x = log_x + end(5, s) + (p * a_s + h * b_s)
            p = end(1, s) + big * (p + span * h)
            h = end(0, s) + big * h
        a, b = nothing, nothing
        for s in reversed(range(SEGS)):
            as_ref[group, s] = rl_rows * a
            b = end(3, s) + big * (b + span * a)
            a = end(2, s) + big * a
        res_sum = lam * res_x + res_near
        log_sum = lam * (log_x + res_x) + log_near
        rows = (h, p, a, b, res_sum, log_sum, jnp.broadcast_to(skip_row, lam.shape), rate)
        for n, value in enumerate(rows):
            pay_ref[pl.ds(n * 8 + group, MODES, stride=64), :] = value
        return carry

    lax.fori_loop(0, groups, group_step, 0)


def chain_kernel(tokens, got_ref, back_ref, skip_ref):
    spans = got_ref.shape[0]

    def part(d, n):
        return got_ref[d, pl.ds(8 * n, 8), :]

    rate = part(0, 7)
    lam = jnp.exp(-rate)
    big = jnp.exp(rate * (-float(tokens)))
    span = float(tokens)
    zero = jnp.zeros((8, LANES), F32)
    h, p, res_x, log_x, res_sum, log_sum, skip = (zero,) * 7
    for d in range(spans):
        back_ref[d, pl.ds(0, 8), :] = h
        a_d = part(d, 2)
        res_x = res_x + h * a_d
        log_x = log_x + (p * a_d + h * part(d, 3))
        res_sum = res_sum + part(d, 4)
        log_sum = log_sum + part(d, 5)
        skip = skip + part(d, 6)
        p = part(d, 1) + big * (p + span * h)
        h = part(d, 0) + big * h
    a = zero
    for d in reversed(range(spans)):
        back_ref[d, pl.ds(8, 8), :] = a
        a = part(d, 2) + big * a
    res_total = res_sum + lam * res_x
    log_total = log_sum + lam * (log_x + res_x)
    for d in range(spans):
        back_ref[d, pl.ds(16, 8), :] = res_total
        back_ref[d, pl.ds(24, 8), :] = log_total
    skip_ref[...] = skip


def put(hbm, buf, sem, group):
    return pltpu.make_async_copy(buf.at[group], hbm.at[:, columns(group)], sem.at[group])


def natural_order(natural, seg_len):
    return jnp.concatenate([natural[pl.ds(s * PITCH, seg_len), :] for s in range(SEGS)], axis=0)


def entering(group, first, back_ref, rows_ref, local_ref, run, backward):
    big = rows_ref[0, group]
    state = rows_ref[1, group] * rows_of(back_ref, first + group, MODES, 32)
    for s in reversed(range(SEGS)) if backward else range(SEGS):
        run[pl.ds(s, MODES, stride=SEGS), :] = local_ref[group, s] + state
        if s != (0 if backward else SEGS - 1):
            state = state * big


def far(total, indices, local_ref, group, k, lam_ref, mu_ref, run):
    for m in range(MODES):
        here = pl.ds(m * SEGS, SEGS)
        step = lam_ref[group, m]
        state = run[here, :]
        c = local_ref[group, k, m] + state
        run[here, :] = state * mu_ref[group, m]
        for i in indices:
            total[i] = total[i] + c
            if i != indices[-1]:
                c = c * step


def back_kernel(
    sq_ref, lam_ref, mu_ref, near_ref, rows_ref, al_ref, as_ref, back_ref,
    ig_hbm,
    natural, run, buf, sem,
):
    groups, tokens, _ = buf.shape
    seg_len = tokens // SEGS
    chunks = seg_len // SUB

    def group_step(group, carry):
        entering(group, 8, back_ref, rows_ref, as_ref, run, True)

        def chunk_step(step, carry):
            k = chunks - 1 - step
            near = [near_ref[group, d] for d in range(SUB)]
            ss = [sq_ref[group, k * SUB + j] for j in range(SUB)]
            total = []
            for j in range(SUB):
                value = near[0] * ss[j]
                for d in range(1, SUB - j):
                    value = value + near[d] * ss[j + d]
                total.append(value)
            far(total, list(reversed(range(SUB))), al_ref, group, k, lam_ref, mu_ref, run)
            for j in range(SUB):
                natural[pl.ds(k * SUB + j, SEGS, stride=PITCH), :] = total[j]
            return carry

        lax.fori_loop(0, chunks, chunk_step, 0)
        buf[group] = natural_order(natural, seg_len).astype(jnp.bfloat16)
        put(ig_hbm, buf, sem, group).start()
        return carry

    lax.fori_loop(0, groups, group_step, 0)
    for group in range(groups):
        put(ig_hbm, buf, sem, group).wait()


def gate_kernel(
    g_hbm, xq_ref, lam_ref, mu_ref, near_ref, rows_ref, hl_ref, hs_ref, back_ref,
    gg_hbm,
    natural, run, g_buf, buf, g_sem, sem,
):
    groups, tokens, _ = buf.shape
    seg_len = tokens // SEGS
    chunks = seg_len // SUB
    for group in range(groups):
        fetch(g_hbm, g_buf, g_sem, group).start()

    def group_step(group, carry):
        entering(group, 0, back_ref, rows_ref, hs_ref, run, False)

        def chunk_step(k, carry):
            near = [near_ref[group, d] for d in range(SUB)]
            xs = [xq_ref[group, k * SUB + j] for j in range(SUB)]
            total = []
            for i in range(SUB):
                value = near[0] * xs[i]
                for d in range(1, i + 1):
                    value = value + near[d] * xs[i - d]
                total.append(value)
            far(total, list(range(SUB)), hl_ref, group, k, lam_ref, mu_ref, run)
            for i in range(SUB):
                natural[pl.ds(k * SUB + i, SEGS, stride=PITCH), :] = total[i]
            return carry

        lax.fori_loop(0, chunks, chunk_step, 0)
        fetch(g_hbm, g_buf, g_sem, group).wait()
        mixed = natural_order(natural, seg_len)
        buf[group] = (g_buf[group].astype(F32) * mixed).astype(jnp.bfloat16)
        put(gg_hbm, buf, sem, group).start()
        return carry

    lax.fori_loop(0, groups, group_step, 0)
    for group in range(groups):
        put(gg_hbm, buf, sem, group).wait()


def totals(back_ref, rows_ref, group):
    res_raw = rows_of(back_ref, 16 + group, MODES, 32)
    log_raw = rows_ref[2, group] * rows_of(back_ref, 24 + group, MODES, 32)
    return res_raw, log_raw


def norm_kernel(back_ref, skip_ref, rows_ref, sq_ref):
    groups = skip_ref.shape[0]
    res_sq = jnp.zeros((MODES, LANES), F32)
    log_sq = jnp.zeros((MODES, LANES), F32)
    for group in range(groups):
        res_raw, log_raw = totals(back_ref, rows_ref, group)
        res_sq = res_sq + res_raw * res_raw
        log_sq = log_sq + log_raw * log_raw
    skip = skip_ref[...]
    rows = [jnp.sum(v, axis=0, keepdims=True) for v in (res_sq, log_sq, skip * skip)]
    sq_ref[...] = jnp.concatenate(rows + [jnp.zeros((5, LANES), F32)], axis=0)


def scale_kernel(own_ref, other_ref, back_ref, skip_ref, rows_ref, rg_ref, lg_ref, sg_ref):
    groups = skip_ref.shape[0]
    sums = jnp.sum(own_ref[...] + other_ref[...], axis=1, keepdims=True)

    def factor(n, ceiling):
        return jnp.minimum(1.0, ceiling / jnp.sqrt(sums[n : n + 1, :] + 1e-06))

    limit_modes = math.sqrt(MODES * CHANNELS)
    res_factor = factor(0, limit_modes)
    log_factor = factor(1, limit_modes)
    for group in range(groups):
        cols = pl.ds(group * LANES, LANES)
        res_raw, log_raw = totals(back_ref, rows_ref, group)
        rg_ref[:, cols] = res_raw * res_factor
        lg_ref[:, cols] = log_raw * log_factor
    sg_ref[...] = skip_ref[...] * factor(2, math.sqrt(CHANNELS))


def params():
    return pltpu.CompilerParams(vmem_limit_bytes=VMEM_LIMIT)


def work(ops, moved):
    return pl.CostEstimate(flops=ops, bytes_accessed=moved, transcendentals=0)


HBM = pl.BlockSpec(memory_space=pltpu.HBM)
VMEM = pl.BlockSpec(memory_space=pltpu.VMEM)


def in_hbm(*arrays):
    return [pltpu.with_memory_space_constraint(array, pltpu.HBM) for array in arrays]


def shape(*dims):
    return jax.ShapeDtypeStruct(dims, F32)


def span_call(conv_input, out_gate, grad_out, pole_rate, residue, skip_gain):
    tokens, chan = conv_input.shape
    groups = chan // LANES
    seg_len = tokens // SEGS
    chunks = seg_len // SUB
    wide = pltpu.VMEM((groups, tokens, LANES), jnp.bfloat16)
    natural = pltpu.VMEM((SEGS * PITCH, LANES), F32)
    sems = pltpu.SemaphoreType.DMA((groups,))
    return pl.pallas_call(
        span_kernel,
        in_specs=[HBM] * 6,
        out_specs=[VMEM] * 11,
        out_shape=[
            shape(groups, chunks, MODES, SEGS, LANES),
            shape(groups, chunks, MODES, SEGS, LANES),
            shape(groups, SEGS, MODES, LANES),
            shape(groups, SEGS, MODES, LANES),
            shape(groups, seg_len, SEGS, LANES),
            shape(groups, seg_len, SEGS, LANES),
            shape(groups, MODES, SEGS, LANES),
            shape(groups, MODES, SEGS, LANES),
            shape(groups, SUB, SEGS, LANES),
            shape(3, groups, MODES, LANES),
            shape(MODES * 64, LANES),
        ],
        scratch_shapes=[
            wide, wide, wide,
            pltpu.VMEM((MODES, chan), F32),
            pltpu.VMEM((MODES, chan), F32),
            pltpu.VMEM((1, chan), F32),
            natural, natural,
            pltpu.VMEM((MODES, SEGS, LANES), F32),
            pltpu.VMEM((6, MODES * SEGS, LANES), F32),
            sems, sems, sems, pltpu.SemaphoreType.DMA((3,)),
        ],
        compiler_params=params(),
        name="span",
    )(
        *in_hbm(conv_input, out_gate, grad_out, pole_rate, residue, skip_gain.reshape(1, chan))
    )


def back_call(tokens, chan, sq, lam, mu, near, rows, al, as_, back):
    groups = chan // LANES
    return pl.pallas_call(
        back_kernel,
        in_specs=[VMEM] * 8,
        out_specs=HBM,
        out_shape=jax.ShapeDtypeStruct((tokens, chan), jnp.bfloat16),
        scratch_shapes=[
            pltpu.VMEM((SEGS * PITCH, LANES), F32),
            pltpu.VMEM((MODES * SEGS, LANES), F32),
            pltpu.VMEM((groups, tokens, LANES), jnp.bfloat16),
            pltpu.SemaphoreType.DMA((groups,)),
        ],
        compiler_params=params(),
        cost_estimate=work(40 * MODES * tokens * chan, 16 * tokens * chan),
        name="adjoint",
    )(sq, lam, mu, near, rows, al, as_, back)


def gate_call(grad_out, xq, lam, mu, near, rows, hl, hs, back):
    tokens, chan = grad_out.shape
    groups = chan // LANES
    wide = pltpu.VMEM((groups, tokens, LANES), jnp.bfloat16)
    sems = pltpu.SemaphoreType.DMA((groups,))
    return pl.pallas_call(
        gate_kernel,
        in_specs=[HBM] + [VMEM] * 8,
        out_specs=HBM,
        out_shape=jax.ShapeDtypeStruct((tokens, chan), jnp.bfloat16),
        scratch_shapes=[
            pltpu.VMEM((SEGS * PITCH, LANES), F32),
            pltpu.VMEM((MODES * SEGS, LANES), F32),
            wide, wide, sems, sems,
        ],
        compiler_params=params(),
        cost_estimate=work(40 * MODES * tokens * chan, 16 * tokens * chan),
        name="gate",
    )(*in_hbm(grad_out), xq, lam, mu, near, rows, hl, hs, back)


def outs_call(conv_input, out_gate, grad_out, made, back):
    hl, al, hs, as_, xq, sq, lam, mu, near, rows = made
    tokens, chan = conv_input.shape
    return (
        back_call(tokens, chan, sq, lam, mu, near, rows, al, as_, back),
        gate_call(grad_out, xq, lam, mu, near, rows, hl, hs, back),
    )


def swapped(value, bit):
    peers = lax.axis_size("ch")
    return lax.ppermute(value, "ch", [(i, i ^ bit) for i in range(peers)])


def on_device(conv_input, out_gate, grad_out, pole_rate, residue, skip_gain):
    tokens, chan = conv_input.shape
    groups = chan // LANES
    spans = lax.axis_size("ctx")
    *made, pay = span_call(conv_input, out_gate, grad_out, pole_rate, residue, skip_gain)
    rows = made[9]
    got = lax.all_to_all(pay.reshape(spans, 64, LANES), "ctx", 0, 0)
    back, skip_raw = pl.pallas_call(
        functools.partial(chain_kernel, tokens),
        out_shape=[
            jax.ShapeDtypeStruct((spans, 32, LANES), F32),
            jax.ShapeDtypeStruct((groups, LANES), F32),
        ],
        compiler_params=params(),
        name="chain",
    )(got)
    back = lax.all_to_all(back, "ctx", 0, 0).reshape(MODES * 32, LANES)

    squares = pl.pallas_call(
        norm_kernel,
        out_shape=shape(8, LANES),
        compiler_params=params(),
        name="norm",
    )(back, skip_raw, rows)
    first = swapped(squares, 2)
    input_grad, gate_grad = outs_call(conv_input, out_gate, grad_out, made, back)
    first, input_grad = lax.optimization_barrier((first, input_grad))
    squares = squares + first
    second = swapped(squares, 4)
    second, gate_grad = lax.optimization_barrier((second, gate_grad))
    squares = squares + second
    other = swapped(squares, 1)
    res_out, log_out, skip_out = pl.pallas_call(
        scale_kernel,
        out_shape=[shape(MODES, chan), shape(MODES, chan), shape(groups, LANES)],
        compiler_params=params(),
        name="scale",
    )(squares, other, back, skip_raw, rows)
    return input_grad, gate_grad, res_out, log_out, skip_out.reshape(chan)


def solution(mesh):
    in_specs = (
        P("ctx", "ch"), P("ctx", "ch"), P("ctx", "ch"), P(None, "ch"), P(None, "ch"), P("ch"),
    )
    out_specs = (P("ctx", "ch"), P("ctx", "ch"), P(None, "ch"), P(None, "ch"), P("ch"))
    return jax.shard_map(
        on_device, mesh=mesh, in_specs=in_specs, out_specs=out_specs, check_vma=False
    )
```

profile of v0, /device:TPU:1, one launch (start us, length us, event | category | flops | bytes accessed | tf_op | source)
XLA Modules:
  0.0 63.8 jit_solution(13488980275349432750)
XLA Ops:
  0.6 14.6 %span.1 = (f32[8,8,16,8,128]{4,3,2,1,0:T(8,128)S(1)}, f32[8,8,16,8,128]{4,3,2,1,0:T(8,128)S(1)}, f32[8,8,16,128]{3,2,1,0:T(8,128)S(1)}, f32[8,8,16,128]{3,2,1,0:...) custom-call(bf16[512,1024]{1,0:T(8,128)(2,1)} %x_hbm.1, ...), custom_call_target="tpu_custom_call" | custom-call | tf_op jit(solution)/shard_map/span/pallas_call | solution.py:412
  15.3 18.5 %all_to_all.10.got_ref = f32[16,64,128]{2,1,0:T(8,128)S(1)} all-to-all(f32[16,64,128]{2,1,0:T(8,128)S(1)} %bitcast.8), channel_id=1, replica_groups=mesh['ctx'=16,'ch'=8] {'ctx'}, dimensions={0} | all-to-all | bytes 1048576 | tf_op jit(solution)/shard_map/all_to_all | solution.py:506
  33.8 0.1 chain.1
  33.9 10.7 %all_to_all.11 = f32[16,32,128]{2,1,0:T(8,128)S(1)} all-to-all(f32[16,32,128]{2,1,0:T(8,128)S(1)} %get-tuple-element.26), channel_id=1, replica_groups=mesh['ctx'=16,'ch'=8] {'ctx'}, dimensions={0} | all-to-all | bytes 524288 | tf_op jit(solution)/shard_map/all_to_all | solution.py:516
  44.5 0.1 norm.1
  44.6 1.4 %collective-permute-start = (f32[8,128]{1,0:T(8,128)S(1)}, f32[8,128]{1,0:T(8,128)S(1)}, u32[]{:S(2)}, u32[]{:S(2)}) collective-permute-start(f32[8,128]{1,0:T(8,128)S(1)} %norm.1), channel_id=1, source_target_pairs={{0,2},{1,3},{2,0},{3,1},{4,6},{5,7},{6,4},{7,5},{8,10},{9,11},{10,... | collective-permute-start | bytes 12296 | tf_op jit(solution)/shard_map/ppermute | solution.py:497
  46.0 4.6 %adjoint.1 = bf16[512,1024]{1,0:T(8,128)(2,1)} custom-call(f32[8,64,8,128]{3,2,1,0:T(8,128)S(1)} %get-tuple-element.29.sq_ref, f32[8,16,8,128]{3,2,1,0:T(8,128)S(1)} %get-tuple-element.30.lam_ref, f32[8,16,8,128]{3,2,1,0:T(8,128)S(1)} %get-tuple-element.31.mu_ref, f32[8,8,8,128]{3,2,1,0:T(8,128)S(1)} %get-tuple-element.32.near_ref, ...), custom_call_target="tpu_custom_call" | custom-call | flops 335544320 | bytes 8388608 | tf_op jit(solution)/shard_map/adjoint/pallas_call | solution.py:448
  50.6 0.0 collective-permute-done
  50.6 2.7 %collective-permute-start.1 = (f32[8,128]{1,0:T(8,128)S(1)}, f32[8,128]{1,0:T(8,128)S(1)}, u32[]{:S(2)}, u32[]{:S(2)}) collective-permute-start(f32[8,128]{1,0:T(8,128)S(1)} %add.6), channel_id=1, source_target_pairs={{0,4},{1,5},{2,6},{3,7},{4,0},{5,1},{6,2},{7,3},{8,12},{9,13},{10,... | collective-permute-start | bytes 12296 | tf_op jit(solution)/shard_map/ppermute | solution.py:497
  53.3 5.1 %gate.1 = bf16[512,1024]{1,0:T(8,128)(2,1)} custom-call(bf16[512,1024]{1,0:T(8,128)(2,1)} %g_hbm.3, f32[8,64,8,128]{3,2,1,0:T(8,128)S(1)} %get-tuple-element.37.xq_ref, f32[8,16,8,128]{3,2,1,0:T(8,128)S(1)} %get-tuple-element.30.lam_ref, f32[8,16,8,128]{3,2,1,0:T(8,128)S(1)} %get-tuple-element.31.mu_ref, f32[8,8,8,128]{3,2,1,0:T(8,128)S(1)} %get-tuple-element.32.near_ref, ...), custom_call_target="tpu_custom_call" | custom-call | flops 335544320 | bytes 8388608 | tf_op jit(solution)/shard_map/gate/pallas_call | solution.py:470
  58.4 0.0 collective-permute-done.1
  58.4 3.9 %collective-permute-start.2 = (f32[8,128]{1,0:T(8,128)S(1)}, f32[8,128]{1,0:T(8,128)S(1)}, u32[]{:S(2)}, u32[]{:S(2)}) collective-permute-start(f32[8,128]{1,0:T(8,128)S(1)} %add.7.own_ref), channel_id=1, source_target_pairs={{0,1},{1,0},{2,3},{3,2},{4,5},{5,4},{6,7},{7,6},{8,9},{9,8},{10,11... | collective-permute-start | bytes 12296 | tf_op jit(solution)/shard_map/ppermute | solution.py:497
  62.3 0.8 %collective-permute-done.2.other_ref = f32[8,128]{1,0:T(8,128)S(1)} collective-permute-done((f32[8,128]{1,0:T(8,128)S(1)}, f32[8,128]{1,0:T(8,128)S(1)}, u32[]{:S(2)}, u32[]{:S(2)}) %collective-permute-start.2) | collective-permute-done | bytes 4128 | tf_op jit(solution)/shard_map/ppermute | solution.py:497
  63.1 0.8 %scale.1 = (f32[16,1024]{1,0:T(8,128)}, f32[16,1024]{1,0:T(8,128)}, f32[8,128]{1,0:T(8,128)}) custom-call(f32[8,128]{1,0:T(8,128)S(1)} %add.7.own_ref, f32[8,128]{1,0:T(8,128)S(1)} %collective-permute-done.2.other_ref, f32[512,128]{1,0:T(8,128)S(1)} %bitcast.7, f32[8,128]{1,0:T(8,128)S(1)} %get-tuple-element.27.skip_ref, ...), custom_call_target="tpu_custom_call" | custom-call | tf_op jit(solution)/shard_map/scale/pallas_call | solution.py:532
  (2 shorter events, 0.0 us)
Async XLA Ops:
  44.6 6.0 %collective-permute-start = (f32[8,128]{1,0:T(8,128)S(1)}, f32[8,128]{1,0:T(8,128)S(1)}, u32[]{:S(2)}, u32[]{:S(2)}) collective-permute-start(f32[8,128]{1,0:T(8,128)S(1)} %norm.1), channel_id=1, source_target_pairs={{0,2},{1,3},{2,0},{3,1},{4,6},{5,7},{6,4},{7,5},{8,10},{9,11},{10,... | collective-permute-start | bytes 12296 | tf_op jit(solution)/shard_map/ppermute | solution.py:497
  50.6 7.8 %collective-permute-start.1 = (f32[8,128]{1,0:T(8,128)S(1)}, f32[8,128]{1,0:T(8,128)S(1)}, u32[]{:S(2)}, u32[]{:S(2)}) collective-permute-start(f32[8,128]{1,0:T(8,128)S(1)} %add.6), channel_id=1, source_target_pairs={{0,4},{1,5},{2,6},{3,7},{4,0},{5,1},{6,2},{7,3},{8,12},{9,13},{10,... | collective-permute-start | bytes 12296 | tf_op jit(solution)/shard_map/ppermute | solution.py:497
  58.4 4.7 %collective-permute-start.2 = (f32[8,128]{1,0:T(8,128)S(1)}, f32[8,128]{1,0:T(8,128)S(1)}, u32[]{:S(2)}, u32[]{:S(2)}) collective-permute-start(f32[8,128]{1,0:T(8,128)S(1)} %add.7.own_ref), channel_id=1, source_target_pairs={{0,1},{1,0},{2,3},{3,2},{4,5},{5,4},{6,7},{7,6},{8,9},{9,8},{10,11... | collective-permute-start | bytes 12296 | tf_op jit(solution)/shard_map/ppermute | solution.py:497
where the time goes:
time: 64.1 us; the launch traced here: 63.8 us
  blocking collectives  29.2 us (46%)
  Pallas kernels  25.2 us (39%)
  starting transfers between devices  7.96 us (12%)
  waiting for transfers between devices  0.83 us (1%)
  between operations  0.69 us (1%)
    all_to_all x1, blocking collectives, on_device(): got = lax.all_to_all(pay.reshape(spans, 64, LANES), 'ctx', 0, 0)  18.5 us
    pallas_call x1, Pallas kernels, span_call(): pl.pallas_call(span_kernel, in_specs=[HBM] * 6, out_specs=[VMEM] * 11, ou...  14.6 us
    all_to_all x1, blocking collectives, on_device(): back = lax.all_to_all(back, 'ctx', 0, 0).reshape(MODES * 32, LANES)  10.7 us
    ppermute x3, starting transfers between devices, swapped(): return lax.ppermute(value, 'ch', [(i, i ^ bit) for i in range(peers)])  7.96 us
    pallas_call x1, Pallas kernels, gate_call(): pl.pallas_call(gate_kernel, in_specs=[HBM] + [VMEM] * 8, out_specs=HBM, o...  5.05 us
    pallas_call x1, Pallas kernels, back_call(): pl.pallas_call(back_kernel, in_specs=[VMEM] * 8, out_specs=HBM, out_shape...  4.57 us
  transfers between devices with their start and end apart: 3, of which 1 were waited for; matrix products, arithmetic and copies ran while one was open for 0% of the time, Pallas kernels for 15%

commit v1 on v0

--- a/solution.py
+++ b/solution.py
@@ -14,8 +14,10 @@
 SEGS = 8
 SUB = 8
 F32 = jnp.float32
+AHEAD = 2
+END_PITCH = 9
 PITCH = 72
-VMEM_LIMIT = 24 * 1024 * 1024
+VMEM_LIMIT = 16 * 1024 * 1024
 
 
 def rows_of(ref, start, count, stride):
@@ -30,25 +32,15 @@
     return pl.ds(pl.multiple_of(group * LANES, LANES), LANES)
 
 
-def fetch(hbm, buf, sem, group):
-    return pltpu.make_async_copy(hbm.at[:, columns(group)], buf.at[group], sem.at[group])
-
-
-def order(natural, ordered, values, seg_len):
-    for s in range(SEGS):
-        natural[pl.ds(s * PITCH, seg_len), :] = values[s * seg_len : (s + 1) * seg_len]
-    for q in range(seg_len):
-        ordered[q] = rows_of(natural, q, SEGS, PITCH)
-
-
 def span_kernel(
     x_hbm, o_hbm, g_hbm, rate_hbm, res_hbm, gain_hbm,
-    hl_ref, al_ref, hs_ref, as_ref, xq_ref, sq_ref, lam_ref, mu_ref, near_ref, rows_ref, pay_ref,
-    x_buf, o_buf, g_buf, rate_buf, res_buf, gain_buf,
+    hl_ref, al_ref, hs_ref, as_ref, xq_ref, sq_ref, lam_ref, mu_ref, near_ref, rows_ref, pay_ref, g_buf,
+    x_buf, o_buf, rate_buf, res_buf, gain_buf,
     natural, second, rl_t, ends,
     x_sem, o_sem, g_sem, small_sem,
 ):
-    groups, tokens, _ = x_buf.shape
+    tokens = x_buf.shape[1]
+    groups = xq_ref.shape[0]
     seg_len = tokens // SEGS
     chunks = seg_len // SUB
     small = [
@@ -57,17 +49,34 @@
             ((rate_hbm, rate_buf), (res_hbm, res_buf), (gain_hbm, gain_buf))
         )
     ]
+
+    def blocks(group, slot):
+        return [
+            pltpu.make_async_copy(hbm.at[:, columns(group)], buf, sem.at[slot])
+            for hbm, buf, sem in (
+                (x_hbm, x_buf.at[slot], x_sem),
+                (o_hbm, o_buf.at[slot], o_sem),
+                (g_hbm, g_buf.at[group], g_sem),
+            )
+        ]
+
     for copy in small:
         copy.start()
-    for group in range(groups):
-        fetch(x_hbm, x_buf, x_sem, group).start()
-        fetch(o_hbm, o_buf, o_sem, group).start()
-        fetch(g_hbm, g_buf, g_sem, group).start()
+    for group in range(min(AHEAD, groups)):
+        for copy in blocks(group, group):
+            copy.start()
     for copy in small:
         copy.wait()
     zero = jnp.zeros((SEGS, LANES), F32)
 
     def group_step(group, carry):
+        slot = lax.rem(group, AHEAD + 1)
+
+        @pl.when(group + AHEAD < groups)
+        def _():
+            for copy in blocks(group + AHEAD, lax.rem(group + AHEAD, AHEAD + 1)):
+                copy.start()
+
         cols = columns(group)
         rate = rate_buf[:, cols]
         residue = res_buf[:, cols]
@@ -92,18 +101,24 @@
 
         xq = xq_ref.at[group]
         sq = sq_ref.at[group]
-        fetch(x_hbm, x_buf, x_sem, group).wait()
-        fetch(o_hbm, o_buf, o_sem, group).wait()
-        fetch(g_hbm, g_buf, g_sem, group).wait()
-        source = x_buf[group].astype(F32)
-        signal = g_buf[group].astype(F32) * o_buf[group].astype(F32)
-        skip_row = jnp.sum(source * signal, axis=0, keepdims=True)
-        order(natural, xq, source, seg_len)
-        order(second, sq, signal, seg_len)
+        for copy in blocks(group, slot):
+            copy.wait()
+        skip_sum = zero
+        for s in range(SEGS):
+            part = pl.ds(s * seg_len, seg_len)
+            source = x_buf[slot, part, :].astype(F32)
+            signal = g_buf[group, part, :].astype(F32) * o_buf[slot, part, :].astype(F32)
+            natural[pl.ds(s * PITCH, seg_len), :] = source
+            second[pl.ds(s * PITCH, seg_len), :] = signal
+            skip_sum = skip_sum + jnp.sum((source * signal).reshape(-1, 8, LANES), axis=0)
+        skip_row = jnp.sum(skip_sum, axis=0, keepdims=True)
 
         def lag_step(k, acc):
-            xs = [xq[k * SUB + j] for j in range(SUB)]
-            ss = [sq[k * SUB + j] for j in range(SUB)]
+            xs = [rows_of(natural, k * SUB + j, SEGS, PITCH) for j in range(SUB)]
+            ss = [rows_of(second, k * SUB + j, SEGS, PITCH) for j in range(SUB)]
+            for j in range(SUB):
+                xq[k * SUB + j] = xs[j]
+                sq[k * SUB + j] = ss[j]
             out = []
             for d in range(SUB):
                 total = acc[d]
@@ -112,7 +127,7 @@
                 out.append(total)
             return tuple(out)
 
-        lagged = lax.fori_loop(0, chunks, lag_step, (zero,) * SUB)
+        lagged = lax.fori_loop(0, chunks, lag_step, (zero,) * SUB, unroll=8)
         lag_rows = [jnp.sum(v, axis=0, keepdims=True) for v in lagged]
         res_near = jnp.broadcast_to(lag_rows[0], lam.shape)
         log_near = jnp.zeros_like(lam)
@@ -170,13 +185,13 @@
                 p_run = p + mu * (p_run + float(SUB) * h_run)
                 h_run = h + mu * h_run
             for n, value in enumerate((h_run, p_run, a_run, b_run, res_x, log_x)):
-                ends[n, pl.ds(pl.multiple_of(m * SEGS, SEGS), SEGS), :] = value
+                ends[n, pl.ds(m * END_PITCH, SEGS), :] = value
             return carry
 
-        lax.fori_loop(0, MODES, mode_step, 0)
+        lax.fori_loop(0, MODES, mode_step, 0, unroll=16)
 
         def end(n, s):
-            return ends[n, pl.ds(s, MODES, stride=SEGS), :]
+            return ends[n, pl.ds(s, MODES, stride=END_PITCH), :]
 
         span = float(seg_len)
         nothing = jnp.zeros_like(lam)
@@ -269,10 +284,10 @@
 
 def back_kernel(
     sq_ref, lam_ref, mu_ref, near_ref, rows_ref, al_ref, as_ref, back_ref,
-    ig_hbm,
-    natural, run, buf, sem,
+    ig_ref,
+    natural, run,
 ):
-    groups, tokens, _ = buf.shape
+    groups, tokens, _ = ig_ref.shape
     seg_len = tokens // SEGS
     chunks = seg_len // SUB
 
@@ -294,26 +309,23 @@
                 natural[pl.ds(k * SUB + j, SEGS, stride=PITCH), :] = total[j]
             return carry
 
-        lax.fori_loop(0, chunks, chunk_step, 0)
-        buf[group] = natural_order(natural, seg_len).astype(jnp.bfloat16)
-        put(ig_hbm, buf, sem, group).start()
+        lax.fori_loop(0, chunks, chunk_step, 0, unroll=8)
+        ig_ref[group] = natural_order(natural, seg_len).astype(jnp.bfloat16)
         return carry
 
     lax.fori_loop(0, groups, group_step, 0)
-    for group in range(groups):
-        put(ig_hbm, buf, sem, group).wait()
 
 
 def gate_kernel(
-    g_hbm, xq_ref, lam_ref, mu_ref, near_ref, rows_ref, hl_ref, hs_ref, back_ref,
-    gg_hbm,
-    natural, run, g_buf, buf, g_sem, sem,
+    ig_buf, g_buf, xq_ref, lam_ref, mu_ref, near_ref, rows_ref, hl_ref, hs_ref, back_ref,
+    ig_hbm, gg_hbm,
+    natural, run, buf, ig_sem, sem,
 ):
     groups, tokens, _ = buf.shape
     seg_len = tokens // SEGS
     chunks = seg_len // SUB
     for group in range(groups):
-        fetch(g_hbm, g_buf, g_sem, group).start()
+        put(ig_hbm, ig_buf, ig_sem, group).start()
 
     def group_step(group, carry):
         entering(group, 0, back_ref, rows_ref, hs_ref, run, False)
@@ -332,8 +344,7 @@
                 natural[pl.ds(k * SUB + i, SEGS, stride=PITCH), :] = total[i]
             return carry
 
-        lax.fori_loop(0, chunks, chunk_step, 0)
-        fetch(g_hbm, g_buf, g_sem, group).wait()
+        lax.fori_loop(0, chunks, chunk_step, 0, unroll=8)
         mixed = natural_order(natural, seg_len)
         buf[group] = (g_buf[group].astype(F32) * mixed).astype(jnp.bfloat16)
         put(gg_hbm, buf, sem, group).start()
@@ -341,6 +352,7 @@
 
     lax.fori_loop(0, groups, group_step, 0)
     for group in range(groups):
+        put(ig_hbm, ig_buf, ig_sem, group).wait()
         put(gg_hbm, buf, sem, group).wait()
 
 
@@ -406,13 +418,13 @@
     groups = chan // LANES
     seg_len = tokens // SEGS
     chunks = seg_len // SUB
-    wide = pltpu.VMEM((groups, tokens, LANES), jnp.bfloat16)
+    wide = pltpu.VMEM((AHEAD + 1, tokens, LANES), jnp.bfloat16)
     natural = pltpu.VMEM((SEGS * PITCH, LANES), F32)
-    sems = pltpu.SemaphoreType.DMA((groups,))
+    sems = pltpu.SemaphoreType.DMA((AHEAD + 1,))
     return pl.pallas_call(
         span_kernel,
         in_specs=[HBM] * 6,
-        out_specs=[VMEM] * 11,
+        out_specs=[VMEM] * 12,
         out_shape=[
             shape(groups, chunks, MODES, SEGS, LANES),
             shape(groups, chunks, MODES, SEGS, LANES),
@@ -425,15 +437,16 @@
             shape(groups, SUB, SEGS, LANES),
             shape(3, groups, MODES, LANES),
             shape(MODES * 64, LANES),
+            jax.ShapeDtypeStruct((groups, tokens, LANES), jnp.bfloat16),
         ],
         scratch_shapes=[
-            wide, wide, wide,
+            wide, wide,
             pltpu.VMEM((MODES, chan), F32),
             pltpu.VMEM((MODES, chan), F32),
             pltpu.VMEM((1, chan), F32),
             natural, natural,
             pltpu.VMEM((MODES, SEGS, LANES), F32),
-            pltpu.VMEM((6, MODES * SEGS, LANES), F32),
+            pltpu.VMEM((6, MODES * END_PITCH, LANES), F32),
             sems, sems, sems, pltpu.SemaphoreType.DMA((3,)),
         ],
         compiler_params=params(),
@@ -443,53 +456,42 @@
     )
 
 
-def back_call(tokens, chan, sq, lam, mu, near, rows, al, as_, back):
-    groups = chan // LANES
+def back_call(tokens, sq, lam, mu, near, rows, al, as_, back):
+    groups = sq.shape[0]
     return pl.pallas_call(
         back_kernel,
         in_specs=[VMEM] * 8,
-        out_specs=HBM,
-        out_shape=jax.ShapeDtypeStruct((tokens, chan), jnp.bfloat16),
+        out_specs=VMEM,
+        out_shape=jax.ShapeDtypeStruct((groups, tokens, LANES), jnp.bfloat16),
+        scratch_shapes=[
+            pltpu.VMEM((SEGS * PITCH, LANES), F32),
+            pltpu.VMEM((MODES * SEGS, LANES), F32),
+        ],
+        compiler_params=params(),
+        cost_estimate=work(40 * MODES * tokens * groups * LANES, 16 * tokens * groups * LANES),
+        name="adjoint",
+    )(sq, lam, mu, near, rows, al, as_, back)
+
+
+def gate_call(ig, g, xq, lam, mu, near, rows, hl, hs, back):
+    groups, tokens, _ = g.shape
+    chan = groups * LANES
+    sems = pltpu.SemaphoreType.DMA((groups,))
+    return pl.pallas_call(
+        gate_kernel,
+        in_specs=[VMEM] * 10,
+        out_specs=[HBM] * 2,
+        out_shape=[jax.ShapeDtypeStruct((tokens, chan), jnp.bfloat16)] * 2,
         scratch_shapes=[
             pltpu.VMEM((SEGS * PITCH, LANES), F32),
             pltpu.VMEM((MODES * SEGS, LANES), F32),
             pltpu.VMEM((groups, tokens, LANES), jnp.bfloat16),
-            pltpu.SemaphoreType.DMA((groups,)),
-        ],
-        compiler_params=params(),
-        cost_estimate=work(40 * MODES * tokens * chan, 16 * tokens * chan),
-        name="adjoint",
-    )(sq, lam, mu, near, rows, al, as_, back)
-
-
-def gate_call(grad_out, xq, lam, mu, near, rows, hl, hs, back):
-    tokens, chan = grad_out.shape
-    groups = chan // LANES
-    wide = pltpu.VMEM((groups, tokens, LANES), jnp.bfloat16)
-    sems = pltpu.SemaphoreType.DMA((groups,))
-    return pl.pallas_call(
-        gate_kernel,
-        in_specs=[HBM] + [VMEM] * 8,
-        out_specs=HBM,
-        out_shape=jax.ShapeDtypeStruct((tokens, chan), jnp.bfloat16),
-        scratch_shapes=[
-            pltpu.VMEM((SEGS * PITCH, LANES), F32),
-            pltpu.VMEM((MODES * SEGS, LANES), F32),
-            wide, wide, sems, sems,
+            sems, sems,
         ],
         compiler_params=params(),
         cost_estimate=work(40 * MODES * tokens * chan, 16 * tokens * chan),
         name="gate",
-    )(*in_hbm(grad_out), xq, lam, mu, near, rows, hl, hs, back)
-
-
-def outs_call(conv_input, out_gate, grad_out, made, back):
-    hl, al, hs, as_, xq, sq, lam, mu, near, rows = made
-    tokens, chan = conv_input.shape
-    return (
-        back_call(tokens, chan, sq, lam, mu, near, rows, al, as_, back),
-        gate_call(grad_out, xq, lam, mu, near, rows, hl, hs, back),
-    )
+    )(ig, g, xq, lam, mu, near, rows, hl, hs, back)
 
 
 def swapped(value, bit):
@@ -501,15 +503,13 @@
     tokens, chan = conv_input.shape
     groups = chan // LANES
     spans = lax.axis_size("ctx")
-    *made, pay = span_call(conv_input, out_gate, grad_out, pole_rate, residue, skip_gain)
-    rows = made[9]
+    hl, al, hs, as_, xq, sq, lam, mu, near, rows, pay, g = span_call(
+        conv_input, out_gate, grad_out, pole_rate, residue, skip_gain
+    )
     got = lax.all_to_all(pay.reshape(spans, 64, LANES), "ctx", 0, 0)
     back, skip_raw = pl.pallas_call(
         functools.partial(chain_kernel, tokens),
-        out_shape=[
-            jax.ShapeDtypeStruct((spans, 32, LANES), F32),
-            jax.ShapeDtypeStruct((groups, LANES), F32),
-        ],
+        out_shape=[shape(spans, 32, LANES), shape(groups, LANES)],
         compiler_params=params(),
         name="chain",
     )(got)
@@ -522,11 +522,12 @@
         name="norm",
     )(back, skip_raw, rows)
     first = swapped(squares, 2)
-    input_grad, gate_grad = outs_call(conv_input, out_gate, grad_out, made, back)
-    first, input_grad = lax.optimization_barrier((first, input_grad))
+    ig = back_call(tokens, sq, lam, mu, near, rows, al, as_, back)
+    first, ig = lax.optimization_barrier((first, ig))
     squares = squares + first
     second = swapped(squares, 4)
-    second, gate_grad = lax.optimization_barrier((second, gate_grad))
+    input_grad, gate_grad = gate_call(ig, g, xq, lam, mu, near, rows, hl, hs, back)
+    second, input_grad, gate_grad = lax.optimization_barrier((second, input_grad, gate_grad))
     squares = squares + second
     other = swapped(squares, 1)
     res_out, log_out, skip_out = pl.pallas_call(

time: 64.1 us -> 58.6 us (0.914)
  Pallas kernels: 25.2 us -> 19.7 us
    pallas_call x4, Pallas kernels: 24.3 us -> 18.8 us  [the longest x1 11.4 us: span_call(): pl.pallas_call(span_kernel, in_specs=[HBM] * 6, out_specs=[VMEM] * 12, ou...]
  transfers between devices with their start and end apart: 3 -> 3, of which waited for: 1 -> 1; matrix products, arithmetic and copies ran while one was open for 0% -> 0% of each run, Pallas kernels for 15% -> 13%
where the time goes in v1:
time: 58.6 us; the launch traced here: 58.3 us
  blocking collectives  29.2 us (50%)
  Pallas kernels  19.7 us (34%)
  starting transfers between devices  7.96 us (14%)
  waiting for transfers between devices  0.83 us (1%)
  between operations  0.69 us (1%)
    all_to_all x1, blocking collectives, on_device(): got = lax.all_to_all(pay.reshape(spans, 64, LANES), 'ctx', 0, 0)  18.5 us
    pallas_call x1, Pallas kernels, span_call(): pl.pallas_call(span_kernel, in_specs=[HBM] * 6, out_specs=[VMEM] * 12, ou...  11.4 us
    all_to_all x1, blocking collectives, on_device(): back = lax.all_to_all(back, 'ctx', 0, 0).reshape(MODES * 32, LANES)  10.7 us
    ppermute x3, starting transfers between devices, swapped(): return lax.ppermute(value, 'ch', [(i, i ^ bit) for i in range(peers)])  7.96 us
    pallas_call x1, Pallas kernels, gate_call(): pl.pallas_call(gate_kernel, in_specs=[VMEM] * 10, out_specs=[HBM] * 2, ou...  4.16 us
    pallas_call x1, Pallas kernels, back_call(): pl.pallas_call(back_kernel, in_specs=[VMEM] * 8, out_specs=VMEM, out_shap...  3.19 us
  transfers between devices with their start and end apart: 3, of which 1 were waited for; matrix products, arithmetic and copies ran while one was open for 0% of the time, Pallas kernels for 13%

profile of v1, /device:TPU:1, one launch (start us, length us, event | category | flops | bytes accessed | tf_op | source)
XLA Modules:
  0.0 58.3 jit_solution(8074211063816153937)
XLA Ops:
  0.6 11.4 %span.1 = (f32[8,8,16,8,128]{4,3,2,1,0:T(8,128)S(1)}, f32[8,8,16,8,128]{4,3,2,1,0:T(8,128)S(1)}, f32[8,8,16,128]{3,2,1,0:T(8,128)S(1)}, f32[8,8,16,128]{3,2,1,0:...) custom-call(bf16[512,1024]{1,0:T(8,128)(2,1)} %x_hbm.1, ...), custom_call_target="tpu_custom_call" | custom-call | tf_op jit(solution)/shard_map/span/pallas_call | solution.py:424
  12.1 18.5 %all_to_all.10.got_ref = f32[16,64,128]{2,1,0:T(8,128)S(1)} all-to-all(f32[16,64,128]{2,1,0:T(8,128)S(1)} %bitcast.8), channel_id=1, replica_groups=mesh['ctx'=16,'ch'=8] {'ctx'}, dimensions={0} | all-to-all | bytes 1048576 | tf_op jit(solution)/shard_map/all_to_all | solution.py:509
  30.6 0.1 chain.1
  30.7 10.7 %all_to_all.11 = f32[16,32,128]{2,1,0:T(8,128)S(1)} all-to-all(f32[16,32,128]{2,1,0:T(8,128)S(1)} %get-tuple-element.30), channel_id=1, replica_groups=mesh['ctx'=16,'ch'=8] {'ctx'}, dimensions={0} | all-to-all | bytes 524288 | tf_op jit(solution)/shard_map/all_to_all | solution.py:516
  41.3 0.1 norm.1
  41.4 1.4 %collective-permute-start = (f32[8,128]{1,0:T(8,128)S(1)}, f32[8,128]{1,0:T(8,128)S(1)}, u32[]{:S(2)}, u32[]{:S(2)}) collective-permute-start(f32[8,128]{1,0:T(8,128)S(1)} %norm.1), channel_id=1, source_target_pairs={{0,2},{1,3},{2,0},{3,1},{4,6},{5,7},{6,4},{7,5},{8,10},{9,11},{10,... | collective-permute-start | bytes 12296 | tf_op jit(solution)/shard_map/ppermute | solution.py:499
  42.8 3.2 %adjoint.1.ig_buf = bf16[8,512,128]{2,1,0:T(8,128)(2,1)S(1)} custom-call(f32[8,64,8,128]{3,2,1,0:T(8,128)S(1)} %get-tuple-element.33.sq_ref, f32[8,16,8,128]{3,2,1,0:T(8,128)S(1)} %get-tuple-element.34.lam_ref, f32[8,16,8,128]{3,2,1,0:T(8,128)S(1)} %get-tuple-element.35.mu_ref, f32[8,8,8,128]{3,2,1,0:T(8,128)S(1)} %get-tuple-element.36.near_ref, ...), custom_call_target="tpu_custom_call" | custom-call | flops 335544320 | bytes 8388608 | tf_op jit(solution)/shard_map/adjoint/pallas_call | solution.py:461
  46.0 0.0 collective-permute-done
  46.0 2.7 %collective-permute-start.1 = (f32[8,128]{1,0:T(8,128)S(1)}, f32[8,128]{1,0:T(8,128)S(1)}, u32[]{:S(2)}, u32[]{:S(2)}) collective-permute-start(f32[8,128]{1,0:T(8,128)S(1)} %add.6), channel_id=1, source_target_pairs={{0,4},{1,5},{2,6},{3,7},{4,0},{5,1},{6,2},{7,3},{8,12},{9,13},{10,... | collective-permute-start | bytes 12296 | tf_op jit(solution)/shard_map/ppermute | solution.py:499
  48.7 4.2 %gate.1 = (bf16[512,1024]{1,0:T(8,128)(2,1)}, bf16[512,1024]{1,0:T(8,128)(2,1)}) custom-call(bf16[8,512,128]{2,1,0:T(8,128)(2,1)S(1)} %adjoint.1.ig_buf, bf16[8,512,128]{2,1,0:T(8,128)(2,1)S(1)} %get-tuple-element.41.g_buf, f32[8,64,8,128]{3,2,1,0:T(8,128)S(1)} %get-tuple-element.42.xq_ref, f32[8,16,8,128]{3,2,1,0:T(8,128)S(1)} %get-tuple-element.34.lam_ref, ...), custom_call_target="tpu_custom_call" | custom-call | flops 335544320 | bytes 8388608 | tf_op jit(solution)/shard_map/gate/pallas_call | solution.py:480
  52.9 0.0 collective-permute-done.1
  52.9 3.9 %collective-permute-start.2 = (f32[8,128]{1,0:T(8,128)S(1)}, f32[8,128]{1,0:T(8,128)S(1)}, u32[]{:S(2)}, u32[]{:S(2)}) collective-permute-start(f32[8,128]{1,0:T(8,128)S(1)} %add.7.own_ref), channel_id=1, source_target_pairs={{0,1},{1,0},{2,3},{3,2},{4,5},{5,4},{6,7},{7,6},{8,9},{9,8},{10,11... | collective-permute-start | bytes 12296 | tf_op jit(solution)/shard_map/ppermute | solution.py:499
  56.8 0.8 %collective-permute-done.2.other_ref = f32[8,128]{1,0:T(8,128)S(1)} collective-permute-done((f32[8,128]{1,0:T(8,128)S(1)}, f32[8,128]{1,0:T(8,128)S(1)}, u32[]{:S(2)}, u32[]{:S(2)}) %collective-permute-start.2) | collective-permute-done | bytes 4128 | tf_op jit(solution)/shard_map/ppermute | solution.py:499
  57.6 0.8 %scale.1 = (f32[16,1024]{1,0:T(8,128)}, f32[16,1024]{1,0:T(8,128)}, f32[8,128]{1,0:T(8,128)}) custom-call(f32[8,128]{1,0:T(8,128)S(1)} %add.7.own_ref, f32[8,128]{1,0:T(8,128)S(1)} %collective-permute-done.2.other_ref, f32[512,128]{1,0:T(8,128)S(1)} %bitcast.7, f32[8,128]{1,0:T(8,128)S(1)} %get-tuple-element.31.skip_ref, ...), custom_call_target="tpu_custom_call" | custom-call | tf_op jit(solution)/shard_map/scale/pallas_call | solution.py:533
  (2 shorter events, 0.0 us)
Async XLA Ops:
  41.4 4.6 %collective-permute-start = (f32[8,128]{1,0:T(8,128)S(1)}, f32[8,128]{1,0:T(8,128)S(1)}, u32[]{:S(2)}, u32[]{:S(2)}) collective-permute-start(f32[8,128]{1,0:T(8,128)S(1)} %norm.1), channel_id=1, source_target_pairs={{0,2},{1,3},{2,0},{3,1},{4,6},{5,7},{6,4},{7,5},{8,10},{9,11},{10,... | collective-permute-start | bytes 12296 | tf_op jit(solution)/shard_map/ppermute | solution.py:499
  46.0 6.9 %collective-permute-start.1 = (f32[8,128]{1,0:T(8,128)S(1)}, f32[8,128]{1,0:T(8,128)S(1)}, u32[]{:S(2)}, u32[]{:S(2)}) collective-permute-start(f32[8,128]{1,0:T(8,128)S(1)} %add.6), channel_id=1, source_target_pairs={{0,4},{1,5},{2,6},{3,7},{4,0},{5,1},{6,2},{7,3},{8,12},{9,13},{10,... | collective-permute-start | bytes 12296 | tf_op jit(solution)/shard_map/ppermute | solution.py:499
  52.9 4.7 %collective-permute-start.2 = (f32[8,128]{1,0:T(8,128)S(1)}, f32[8,128]{1,0:T(8,128)S(1)}, u32[]{:S(2)}, u32[]{:S(2)}) collective-permute-start(f32[8,128]{1,0:T(8,128)S(1)} %add.7.own_ref), channel_id=1, source_target_pairs={{0,1},{1,0},{2,3},{3,2},{4,5},{5,4},{6,7},{7,6},{8,9},{9,8},{10,11... | collective-permute-start | bytes 12296 | tf_op jit(solution)/shard_map/ppermute | solution.py:499

commit v2 on v1

--- a/solution.py
+++ b/solution.py
@@ -16,6 +16,8 @@
 F32 = jnp.float32
 AHEAD = 2
 END_PITCH = 9
+SENT = 48
+BACK = 40
 PITCH = 72
 VMEM_LIMIT = 16 * 1024 * 1024
 
@@ -34,7 +36,7 @@
 
 def span_kernel(
     x_hbm, o_hbm, g_hbm, rate_hbm, res_hbm, gain_hbm,
-    hl_ref, al_ref, hs_ref, as_ref, xq_ref, sq_ref, lam_ref, mu_ref, near_ref, rows_ref, pay_ref, g_buf,
+    hl_ref, al_ref, hs_ref, as_ref, xq_ref, sq_ref, lam_ref, mu_ref, near_ref, rows_ref, skip_ref, pay_ref, g_buf,
     x_buf, o_buf, rate_buf, res_buf, gain_buf,
     natural, second, rl_t, ends,
     x_sem, o_sem, g_sem, small_sem,
@@ -91,6 +93,7 @@
         rows_ref[0, group] = big
         rows_ref[1, group] = rl_rows
         rows_ref[2, group] = -(rate * residue)
+        rows_ref[3, group] = rate
         term = residue
         for d in range(SUB):
             row = jnp.sum(term, axis=0, keepdims=True)
@@ -103,15 +106,12 @@
         sq = sq_ref.at[group]
         for copy in blocks(group, slot):
             copy.wait()
-        skip_sum = zero
         for s in range(SEGS):
             part = pl.ds(s * seg_len, seg_len)
             source = x_buf[slot, part, :].astype(F32)
             signal = g_buf[group, part, :].astype(F32) * o_buf[slot, part, :].astype(F32)
             natural[pl.ds(s * PITCH, seg_len), :] = source
             second[pl.ds(s * PITCH, seg_len), :] = signal
-            skip_sum = skip_sum + jnp.sum((source * signal).reshape(-1, 8, LANES), axis=0)
-        skip_row = jnp.sum(skip_sum, axis=0, keepdims=True)
 
         def lag_step(k, acc):
             xs = [rows_of(natural, k * SUB + j, SEGS, PITCH) for j in range(SUB)]
@@ -129,6 +129,7 @@
 
         lagged = lax.fori_loop(0, chunks, lag_step, (zero,) * SUB, unroll=8)
         lag_rows = [jnp.sum(v, axis=0, keepdims=True) for v in lagged]
+        skip_ref[pl.ds(group, 1), :] = lag_rows[0]
         res_near = jnp.broadcast_to(lag_rows[0], lam.shape)
         log_near = jnp.zeros_like(lam)
         power = lam
@@ -210,26 +211,30 @@
             a = end(2, s) + big * a
         res_sum = lam * res_x + res_near
         log_sum = lam * (log_x + res_x) + log_near
-        rows = (h, p, a, b, res_sum, log_sum, jnp.broadcast_to(skip_row, lam.shape), rate)
+        rows = (h, p, a, b, res_sum, log_sum)
         for n, value in enumerate(rows):
-            pay_ref[pl.ds(n * 8 + group, MODES, stride=64), :] = value
+            pay_ref[pl.ds(n * 8 + group, MODES, stride=SENT), :] = value
         return carry
 
     lax.fori_loop(0, groups, group_step, 0)
 
 
-def chain_kernel(tokens, got_ref, back_ref, skip_ref):
+def chain_kernel(tokens, got_ref, rows_ref, skip_ref, back_ref):
     spans = got_ref.shape[0]
+    groups = skip_ref.shape[0]
+    own = lax.axis_index("ctx")
 
     def part(d, n):
         return got_ref[d, pl.ds(8 * n, 8), :]
 
-    rate = part(0, 7)
+    rate = jnp.concatenate(
+        [rows_ref[3, group, pl.ds(own, 1), :] for group in range(groups)], axis=0
+    )
     lam = jnp.exp(-rate)
     big = jnp.exp(rate * (-float(tokens)))
     span = float(tokens)
     zero = jnp.zeros((8, LANES), F32)
-    h, p, res_x, log_x, res_sum, log_sum, skip = (zero,) * 7
+    h, p, res_x, log_x, res_sum, log_sum = (zero,) * 6
     for d in range(spans):
         back_ref[d, pl.ds(0, 8), :] = h
         a_d = part(d, 2)
@@ -237,7 +242,6 @@
         log_x = log_x + (p * a_d + h * part(d, 3))
         res_sum = res_sum + part(d, 4)
         log_sum = log_sum + part(d, 5)
-        skip = skip + part(d, 6)
         p = part(d, 1) + big * (p + span * h)
         h = part(d, 0) + big * h
     a = zero
@@ -249,7 +253,7 @@
     for d in range(spans):
         back_ref[d, pl.ds(16, 8), :] = res_total
         back_ref[d, pl.ds(24, 8), :] = log_total
-    skip_ref[...] = skip
+        back_ref[d, pl.ds(32, 8), :] = skip_ref[...]
 
 
 def put(hbm, buf, sem, group):
@@ -262,7 +266,7 @@
 
 def entering(group, first, back_ref, rows_ref, local_ref, run, backward):
     big = rows_ref[0, group]
-    state = rows_ref[1, group] * rows_of(back_ref, first + group, MODES, 32)
+    state = rows_ref[1, group] * rows_of(back_ref, first + group, MODES, BACK)
     for s in reversed(range(SEGS)) if backward else range(SEGS):
         run[pl.ds(s, MODES, stride=SEGS), :] = local_ref[group, s] + state
         if s != (0 if backward else SEGS - 1):
@@ -357,26 +361,33 @@
 
 
 def totals(back_ref, rows_ref, group):
-    res_raw = rows_of(back_ref, 16 + group, MODES, 32)
-    log_raw = rows_ref[2, group] * rows_of(back_ref, 24 + group, MODES, 32)
+    res_raw = rows_of(back_ref, 16 + group, MODES, BACK)
+    log_raw = rows_ref[2, group] * rows_of(back_ref, 24 + group, MODES, BACK)
     return res_raw, log_raw
 
 
-def norm_kernel(back_ref, skip_ref, rows_ref, sq_ref):
-    groups = skip_ref.shape[0]
+def skip_total(back_ref):
+    total = back_ref[pl.ds(32, 8), :]
+    for span in range(1, back_ref.shape[0] // BACK):
+        total = total + back_ref[pl.ds(span * BACK + 32, 8), :]
+    return total
+
+
+def norm_kernel(back_ref, rows_ref, sq_ref):
+    groups = rows_ref.shape[1]
     res_sq = jnp.zeros((MODES, LANES), F32)
     log_sq = jnp.zeros((MODES, LANES), F32)
     for group in range(groups):
         res_raw, log_raw = totals(back_ref, rows_ref, group)
         res_sq = res_sq + res_raw * res_raw
         log_sq = log_sq + log_raw * log_raw
-    skip = skip_ref[...]
+    skip = skip_total(back_ref)
     rows = [jnp.sum(v, axis=0, keepdims=True) for v in (res_sq, log_sq, skip * skip)]
     sq_ref[...] = jnp.concatenate(rows + [jnp.zeros((5, LANES), F32)], axis=0)
 
 
-def scale_kernel(own_ref, other_ref, back_ref, skip_ref, rows_ref, rg_ref, lg_ref, sg_ref):
-    groups = skip_ref.shape[0]
+def scale_kernel(own_ref, other_ref, back_ref, rows_ref, rg_ref, lg_ref, sg_ref):
+    groups = rows_ref.shape[1]
     sums = jnp.sum(own_ref[...] + other_ref[...], axis=1, keepdims=True)
 
     def factor(n, ceiling):
@@ -390,7 +401,7 @@
         res_raw, log_raw = totals(back_ref, rows_ref, group)
         rg_ref[:, cols] = res_raw * res_factor
         lg_ref[:, cols] = log_raw * log_factor
-    sg_ref[...] = skip_ref[...] * factor(2, math.sqrt(CHANNELS))
+    sg_ref[...] = skip_total(back_ref) * factor(2, math.sqrt(CHANNELS))
 
 
 def params():
@@ -424,7 +435,7 @@
     return pl.pallas_call(
         span_kernel,
         in_specs=[HBM] * 6,
-        out_specs=[VMEM] * 12,
+        out_specs=[VMEM] * 13,
         out_shape=[
             shape(groups, chunks, MODES, SEGS, LANES),
             shape(groups, chunks, MODES, SEGS, LANES),
@@ -435,8 +446,9 @@
             shape(groups, MODES, SEGS, LANES),
             shape(groups, MODES, SEGS, LANES),
             shape(groups, SUB, SEGS, LANES),
-            shape(3, groups, MODES, LANES),
-            shape(MODES * 64, LANES),
+            shape(4, groups, MODES, LANES),
+            shape(groups, LANES),
+            shape(MODES * SENT, LANES),
             jax.ShapeDtypeStruct((groups, tokens, LANES), jnp.bfloat16),
         ],
         scratch_shapes=[
@@ -503,24 +515,24 @@
     tokens, chan = conv_input.shape
     groups = chan // LANES
     spans = lax.axis_size("ctx")
-    hl, al, hs, as_, xq, sq, lam, mu, near, rows, pay, g = span_call(
+    hl, al, hs, as_, xq, sq, lam, mu, near, rows, skip, pay, g = span_call(
         conv_input, out_gate, grad_out, pole_rate, residue, skip_gain
     )
-    got = lax.all_to_all(pay.reshape(spans, 64, LANES), "ctx", 0, 0)
-    back, skip_raw = pl.pallas_call(
+    got = lax.all_to_all(pay.reshape(spans, SENT, LANES), "ctx", 0, 0)
+    back = pl.pallas_call(
         functools.partial(chain_kernel, tokens),
-        out_shape=[shape(spans, 32, LANES), shape(groups, LANES)],
+        out_shape=shape(spans, BACK, LANES),
         compiler_params=params(),
         name="chain",
-    )(got)
-    back = lax.all_to_all(back, "ctx", 0, 0).reshape(MODES * 32, LANES)
+    )(got, rows, skip)
+    back = lax.all_to_all(back, "ctx", 0, 0).reshape(MODES * BACK, LANES)
 
     squares = pl.pallas_call(
         norm_kernel,
         out_shape=shape(8, LANES),
         compiler_params=params(),
         name="norm",
-    )(back, skip_raw, rows)
+    )(back, rows)
     first = swapped(squares, 2)
     ig = back_call(tokens, sq, lam, mu, near, rows, al, as_, back)
     first, ig = lax.optimization_barrier((first, ig))
@@ -535,7 +547,7 @@
         out_shape=[shape(MODES, chan), shape(MODES, chan), shape(groups, LANES)],
         compiler_params=params(),
         name="scale",
-    )(squares, other, back, skip_raw, rows)
+    )(squares, other, back, rows)
     return input_grad, gate_grad, res_out, log_out, skip_out.reshape(chan)
 
 

time: 58.6 us -> 56.9 us (0.971)
  blocking collectives: 29.2 us -> 28 us
  Pallas kernels: 19.7 us -> 19.1 us
    all_to_all x2, blocking collectives: 29.2 us -> 28 us  [the longest x1 16.5 us: on_device(): got = lax.all_to_all(pay.reshape(spans, SENT, LANES), 'ctx', 0, 0)]
where the time goes in v2:
time: 56.9 us; the launch traced here: 56.7 us
  blocking collectives  28 us (49%)
  Pallas kernels  19.1 us (34%)
  starting transfers between devices  8.01 us (14%)
  waiting for transfers between devices  0.83 us (1%)
  between operations  0.69 us (1%)
    all_to_all x1, blocking collectives, on_device(): got = lax.all_to_all(pay.reshape(spans, SENT, LANES), 'ctx', 0, 0)  16.5 us
    all_to_all x1, blocking collectives, on_device(): back = lax.all_to_all(back, 'ctx', 0, 0).reshape(MODES * BACK, LANES)  11.6 us
    pallas_call x1, Pallas kernels, span_call(): pl.pallas_call(span_kernel, in_specs=[HBM] * 6, out_specs=[VMEM] * 13, ou...  11.1 us
    ppermute x3, starting transfers between devices, swapped(): return lax.ppermute(value, 'ch', [(i, i ^ bit) for i in range(peers)])  8.01 us
    pallas_call x1, Pallas kernels, gate_call(): pl.pallas_call(gate_kernel, in_specs=[VMEM] * 10, out_specs=[HBM] * 2, ou...  4.05 us
    pallas_call x1, Pallas kernels, back_call(): pl.pallas_call(back_kernel, in_specs=[VMEM] * 8, out_specs=VMEM, out_shap...  3.12 us
  transfers between devices with their start and end apart: 3, of which 1 were waited for; matrix products, arithmetic and copies ran while one was open for 0% of the time, Pallas kernels for 13%

profile of v2, /device:TPU:1, one launch (start us, length us, event | category | flops | bytes accessed | tf_op | source)
XLA Modules:
  0.0 56.7 jit_solution(13889364346917630277)
XLA Ops:
  0.6 11.1 %span.1 = (f32[8,8,16,8,128]{4,3,2,1,0:T(8,128)S(1)}, f32[8,8,16,8,128]{4,3,2,1,0:T(8,128)S(1)}, f32[8,8,16,128]{3,2,1,0:T(8,128)S(1)}, f32[8,8,16,128]{3,2,1,0:...) custom-call(bf16[512,1024]{1,0:T(8,128)(2,1)} %x_hbm.1, ...), custom_call_target="tpu_custom_call" | custom-call | tf_op jit(solution)/shard_map/span/pallas_call | solution.py:435
  11.7 16.5 %all_to_all.10.got_ref = f32[16,48,128]{2,1,0:T(8,128)S(1)} all-to-all(f32[16,48,128]{2,1,0:T(8,128)S(1)} %bitcast.8), channel_id=1, replica_groups=mesh['ctx'=16,'ch'=8] {'ctx'}, dimensions={0} | all-to-all | bytes 786432 | tf_op jit(solution)/shard_map/all_to_all | solution.py:521
  28.2 0.1 chain.1
  28.3 11.6 %all_to_all.11 = f32[16,40,128]{2,1,0:T(8,128)S(1)} all-to-all(f32[16,40,128]{2,1,0:T(8,128)S(1)} %chain.1), channel_id=1, replica_groups=mesh['ctx'=16,'ch'=8] {'ctx'}, dimensions={0} | all-to-all | bytes 655360 | tf_op jit(solution)/shard_map/all_to_all | solution.py:528
  39.9 1.4 %collective-permute-start = (f32[8,128]{1,0:T(8,128)S(1)}, f32[8,128]{1,0:T(8,128)S(1)}, u32[]{:S(2)}, u32[]{:S(2)}) collective-permute-start(f32[8,128]{1,0:T(8,128)S(1)} %norm.1), channel_id=1, source_target_pairs={{0,2},{1,3},{2,0},{3,1},{4,6},{5,7},{6,4},{7,5},{8,10},{9,11},{10,... | collective-permute-start | bytes 12296 | tf_op jit(solution)/shard_map/ppermute | solution.py:511
  41.3 3.1 %adjoint.1.ig_buf = bf16[8,512,128]{2,1,0:T(8,128)(2,1)S(1)} custom-call(f32[8,64,8,128]{3,2,1,0:T(8,128)S(1)} %get-tuple-element.31.sq_ref, f32[8,16,8,128]{3,2,1,0:T(8,128)S(1)} %get-tuple-element.32.lam_ref, f32[8,16,8,128]{3,2,1,0:T(8,128)S(1)} %get-tuple-element.33.mu_ref, f32[8,8,8,128]{3,2,1,0:T(8,128)S(1)} %get-tuple-element.34.near_ref, ...), custom_call_target="tpu_custom_call" | custom-call | flops 335544320 | bytes 8388608 | tf_op jit(solution)/shard_map/adjoint/pallas_call | solution.py:473
  44.4 0.0 collective-permute-done
  44.4 2.7 %collective-permute-start.1 = (f32[8,128]{1,0:T(8,128)S(1)}, f32[8,128]{1,0:T(8,128)S(1)}, u32[]{:S(2)}, u32[]{:S(2)}) collective-permute-start(f32[8,128]{1,0:T(8,128)S(1)} %add.6), channel_id=1, source_target_pairs={{0,4},{1,5},{2,6},{3,7},{4,0},{5,1},{6,2},{7,3},{8,12},{9,13},{10,... | collective-permute-start | bytes 12296 | tf_op jit(solution)/shard_map/ppermute | solution.py:511
  47.1 4.1 %gate.1 = (bf16[512,1024]{1,0:T(8,128)(2,1)}, bf16[512,1024]{1,0:T(8,128)(2,1)}) custom-call(bf16[8,512,128]{2,1,0:T(8,128)(2,1)S(1)} %adjoint.1.ig_buf, bf16[8,512,128]{2,1,0:T(8,128)(2,1)S(1)} %get-tuple-element.39.g_buf, f32[8,64,8,128]{3,2,1,0:T(8,128)S(1)} %get-tuple-element.40.xq_ref, f32[8,16,8,128]{3,2,1,0:T(8,128)S(1)} %get-tuple-element.32.lam_ref, ...), custom_call_target="tpu_custom_call" | custom-call | flops 335544320 | bytes 8388608 | tf_op jit(solution)/shard_map/gate/pallas_call | solution.py:492
  51.2 0.0 collective-permute-done.1
  51.2 3.9 %collective-permute-start.2 = (f32[8,128]{1,0:T(8,128)S(1)}, f32[8,128]{1,0:T(8,128)S(1)}, u32[]{:S(2)}, u32[]{:S(2)}) collective-permute-start(f32[8,128]{1,0:T(8,128)S(1)} %add.7.own_ref), channel_id=1, source_target_pairs={{0,1},{1,0},{2,3},{3,2},{4,5},{5,4},{6,7},{7,6},{8,9},{9,8},{10,11... | collective-permute-start | bytes 12296 | tf_op jit(solution)/shard_map/ppermute | solution.py:511
  55.2 0.8 %collective-permute-done.2.other_ref = f32[8,128]{1,0:T(8,128)S(1)} collective-permute-done((f32[8,128]{1,0:T(8,128)S(1)}, f32[8,128]{1,0:T(8,128)S(1)}, u32[]{:S(2)}, u32[]{:S(2)}) %collective-permute-start.2) | collective-permute-done | bytes 4128 | tf_op jit(solution)/shard_map/ppermute | solution.py:511
  56.0 0.8 %scale.1 = (f32[16,1024]{1,0:T(8,128)}, f32[16,1024]{1,0:T(8,128)}, f32[8,128]{1,0:T(8,128)}) custom-call(f32[8,128]{1,0:T(8,128)S(1)} %add.7.own_ref, f32[8,128]{1,0:T(8,128)S(1)} %collective-permute-done.2.other_ref, f32[640,128]{1,0:T(8,128)S(1)} %bitcast.7, f32[4,8,16,128]{3,2,1,0:T(8,128)S(1)} %get-tuple-element.29.rows_ref), custom_call_target="tpu_custom_call" | custom-call | tf_op jit(solution)/shard_map/scale/pallas_call | solution.py:545
  (3 shorter events, 0.1 us)
Async XLA Ops:
  39.9 4.5 %collective-permute-start = (f32[8,128]{1,0:T(8,128)S(1)}, f32[8,128]{1,0:T(8,128)S(1)}, u32[]{:S(2)}, u32[]{:S(2)}) collective-permute-start(f32[8,128]{1,0:T(8,128)S(1)} %norm.1), channel_id=1, source_target_pairs={{0,2},{1,3},{2,0},{3,1},{4,6},{5,7},{6,4},{7,5},{8,10},{9,11},{10,... | collective-permute-start | bytes 12296 | tf_op jit(solution)/shard_map/ppermute | solution.py:511
  44.4 6.8 %collective-permute-start.1 = (f32[8,128]{1,0:T(8,128)S(1)}, f32[8,128]{1,0:T(8,128)S(1)}, u32[]{:S(2)}, u32[]{:S(2)}) collective-permute-start(f32[8,128]{1,0:T(8,128)S(1)} %add.6), channel_id=1, source_target_pairs={{0,4},{1,5},{2,6},{3,7},{4,0},{5,1},{6,2},{7,3},{8,12},{9,13},{10,... | collective-permute-start | bytes 12296 | tf_op jit(solution)/shard_map/ppermute | solution.py:511
  51.2 4.8 %collective-permute-start.2 = (f32[8,128]{1,0:T(8,128)S(1)}, f32[8,128]{1,0:T(8,128)S(1)}, u32[]{:S(2)}, u32[]{:S(2)}) collective-permute-start(f32[8,128]{1,0:T(8,128)S(1)} %add.7.own_ref), channel_id=1, source_target_pairs={{0,1},{1,0},{2,3},{3,2},{4,5},{5,4},{6,7},{7,6},{8,9},{9,8},{10,11... | collective-permute-start | bytes 12296 | tf_op jit(solution)/shard_map/ppermute | solution.py:511

commit v3 on v2

--- a/solution.py
+++ b/solution.py
@@ -14,6 +14,7 @@
 SEGS = 8
 SUB = 8
 F32 = jnp.float32
+LATE = 2
 AHEAD = 2
 END_PITCH = 9
 SENT = 48
@@ -62,9 +63,9 @@
             )
         ]
 
-    for copy in small:
+    for copy in blocks(0, 0) + small:
         copy.start()
-    for group in range(min(AHEAD, groups)):
+    for group in range(1, min(AHEAD, groups)):
         for copy in blocks(group, group):
             copy.start()
     for copy in small:
@@ -322,10 +323,11 @@
 
 def gate_kernel(
     ig_buf, g_buf, xq_ref, lam_ref, mu_ref, near_ref, rows_ref, hl_ref, hs_ref, back_ref,
-    ig_hbm, gg_hbm,
+    ig_hbm, gg_hbm, late_ref,
     natural, run, buf, ig_sem, sem,
 ):
-    groups, tokens, _ = buf.shape
+    groups, tokens, _ = g_buf.shape
+    early = groups - LATE
     seg_len = tokens // SEGS
     chunks = seg_len // SUB
     for group in range(groups):
@@ -350,14 +352,24 @@
 
         lax.fori_loop(0, chunks, chunk_step, 0, unroll=8)
         mixed = natural_order(natural, seg_len)
-        buf[group] = (g_buf[group].astype(F32) * mixed).astype(jnp.bfloat16)
-        put(gg_hbm, buf, sem, group).start()
+        gated = (g_buf[group].astype(F32) * mixed).astype(jnp.bfloat16)
+
+        @pl.when(group < early)
+        def _():
+            buf[group] = gated
+            put(gg_hbm, buf, sem, group).start()
+
+        @pl.when(group >= early)
+        def _():
+            late_ref[group - early] = gated
+
         return carry
 
     lax.fori_loop(0, groups, group_step, 0)
     for group in range(groups):
         put(ig_hbm, ig_buf, ig_sem, group).wait()
-        put(gg_hbm, buf, sem, group).wait()
+        if group < early:
+            put(gg_hbm, buf, sem, group).wait()
 
 
 def totals(back_ref, rows_ref, group):
@@ -386,8 +398,20 @@
     sq_ref[...] = jnp.concatenate(rows + [jnp.zeros((5, LANES), F32)], axis=0)
 
 
-def scale_kernel(own_ref, other_ref, back_ref, rows_ref, rg_ref, lg_ref, sg_ref):
+def scale_kernel(
+    own_ref, other_ref, back_ref, rows_ref, late_ref, part_hbm,
+    rg_hbm, lg_hbm, sg_hbm, gg_hbm,
+    rg_buf, lg_buf, sg_buf, late_sem, sem,
+):
     groups = rows_ref.shape[1]
+    copies = [
+        pltpu.make_async_copy(
+            late_ref.at[n], gg_hbm.at[:, columns(groups - LATE + n)], late_sem.at[n]
+        )
+        for n in range(LATE)
+    ]
+    for copy in copies:
+        copy.start()
     sums = jnp.sum(own_ref[...] + other_ref[...], axis=1, keepdims=True)
 
     def factor(n, ceiling):
@@ -399,9 +423,15 @@
     for group in range(groups):
         cols = pl.ds(group * LANES, LANES)
         res_raw, log_raw = totals(back_ref, rows_ref, group)
-        rg_ref[:, cols] = res_raw * res_factor
-        lg_ref[:, cols] = log_raw * log_factor
-    sg_ref[...] = skip_total(back_ref) * factor(2, math.sqrt(CHANNELS))
+        rg_buf[:, cols] = res_raw * res_factor
+        lg_buf[:, cols] = log_raw * log_factor
+    sg_buf[...] = skip_total(back_ref) * factor(2, math.sqrt(CHANNELS))
+    for n, (buf, hbm) in enumerate(((rg_buf, rg_hbm), (lg_buf, lg_hbm), (sg_buf, sg_hbm))):
+        copy = pltpu.make_async_copy(buf, hbm, sem.at[n])
+        copy.start()
+        copies.append(copy)
+    for copy in copies:
+        copy.wait()
 
 
 def params():
@@ -492,12 +522,16 @@
     return pl.pallas_call(
         gate_kernel,
         in_specs=[VMEM] * 10,
-        out_specs=[HBM] * 2,
-        out_shape=[jax.ShapeDtypeStruct((tokens, chan), jnp.bfloat16)] * 2,
+        out_specs=[HBM, HBM, VMEM],
+        out_shape=[
+            jax.ShapeDtypeStruct((tokens, chan), jnp.bfloat16),
+            jax.ShapeDtypeStruct((tokens, chan), jnp.bfloat16),
+            jax.ShapeDtypeStruct((LATE, tokens, LANES), jnp.bfloat16),
+        ],
         scratch_shapes=[
             pltpu.VMEM((SEGS * PITCH, LANES), F32),
             pltpu.VMEM((MODES * SEGS, LANES), F32),
-            pltpu.VMEM((groups, tokens, LANES), jnp.bfloat16),
+            pltpu.VMEM((groups - LATE, tokens, LANES), jnp.bfloat16),
             sems, sems,
         ],
         compiler_params=params(),
@@ -538,16 +572,29 @@
     first, ig = lax.optimization_barrier((first, ig))
     squares = squares + first
     second = swapped(squares, 4)
-    input_grad, gate_grad = gate_call(ig, g, xq, lam, mu, near, rows, hl, hs, back)
-    second, input_grad, gate_grad = lax.optimization_barrier((second, input_grad, gate_grad))
+    input_grad, gate_grad, late = gate_call(ig, g, xq, lam, mu, near, rows, hl, hs, back)
+    second, late = lax.optimization_barrier((second, late))
     squares = squares + second
     other = swapped(squares, 1)
-    res_out, log_out, skip_out = pl.pallas_call(
+    res_out, log_out, skip_out, gate_grad = pl.pallas_call(
         scale_kernel,
-        out_shape=[shape(MODES, chan), shape(MODES, chan), shape(groups, LANES)],
+        in_specs=[VMEM] * 5 + [HBM],
+        out_specs=[HBM] * 4,
+        out_shape=[
+            shape(MODES, chan), shape(MODES, chan), shape(groups, LANES),
+            jax.ShapeDtypeStruct((tokens, chan), jnp.bfloat16),
+        ],
+        scratch_shapes=[
+            pltpu.VMEM((MODES, chan), F32),
+            pltpu.VMEM((MODES, chan), F32),
+            pltpu.VMEM((groups, LANES), F32),
+            pltpu.SemaphoreType.DMA((LATE,)),
+            pltpu.SemaphoreType.DMA((3,)),
+        ],
+        input_output_aliases={5: 3},
         compiler_params=params(),
         name="scale",
-    )(squares, other, back, rows)
+    )(squares, other, back, rows, late, gate_grad)
     return input_grad, gate_grad, res_out, log_out, skip_out.reshape(chan)
 
 

time: 56.9 us -> 56.4 us (level)
  transfers between devices with their start and end apart: 3 -> 3, of which waited for: 1 -> 1; matrix products, arithmetic and copies ran while one was open for 0% -> 0% of each run, Pallas kernels for 13% -> 12%
where the time goes in v3:
time: 56.4 us; the launch traced here: 56.2 us
  blocking collectives  28 us (50%)
  Pallas kernels  18.6 us (33%)
  starting transfers between devices  8.01 us (14%)
  waiting for transfers between devices  0.83 us (1%)
  between operations  0.69 us (1%)
    all_to_all x1, blocking collectives, on_device(): got = lax.all_to_all(pay.reshape(spans, SENT, LANES), 'ctx', 0, 0)  16.5 us
    all_to_all x1, blocking collectives, on_device(): back = lax.all_to_all(back, 'ctx', 0, 0).reshape(MODES * BACK, LANES)  11.6 us
    pallas_call x1, Pallas kernels, span_call(): pl.pallas_call(span_kernel, in_specs=[HBM] * 6, out_specs=[VMEM] * 13, ou...  11.1 us
    ppermute x3, starting transfers between devices, swapped(): return lax.ppermute(value, 'ch', [(i, i ^ bit) for i in range(peers)])  8.01 us
    pallas_call x1, Pallas kernels, gate_call(): pl.pallas_call(gate_kernel, in_specs=[VMEM] * 10, out_specs=[HBM, HBM, VM...  3.47 us
    pallas_call x1, Pallas kernels, back_call(): pl.pallas_call(back_kernel, in_specs=[VMEM] * 8, out_specs=VMEM, out_shap...  3.12 us
  transfers between devices with their start and end apart: 3, of which 1 were waited for; matrix products, arithmetic and copies ran while one was open for 0% of the time, Pallas kernels for 12%

profile of v3, /device:TPU:1, one launch (start us, length us, event | category | flops | bytes accessed | tf_op | source)
XLA Modules:
  0.0 56.2 jit_solution(9029085748353869266)
XLA Ops:
  0.6 11.1 %span.1 = (f32[8,8,16,8,128]{4,3,2,1,0:T(8,128)S(1)}, f32[8,8,16,8,128]{4,3,2,1,0:T(8,128)S(1)}, f32[8,8,16,128]{3,2,1,0:T(8,128)S(1)}, f32[8,8,16,128]{3,2,1,0:...) custom-call(bf16[512,1024]{1,0:T(8,128)(2,1)} %x_hbm.1, ...), custom_call_target="tpu_custom_call" | custom-call | tf_op jit(solution)/shard_map/span/pallas_call | solution.py:465
  11.7 16.5 %all_to_all.10.got_ref = f32[16,48,128]{2,1,0:T(8,128)S(1)} all-to-all(f32[16,48,128]{2,1,0:T(8,128)S(1)} %bitcast.8), channel_id=1, replica_groups=mesh['ctx'=16,'ch'=8] {'ctx'}, dimensions={0} | all-to-all | bytes 786432 | tf_op jit(solution)/shard_map/all_to_all | solution.py:555
  28.2 0.1 chain.1
  28.3 11.6 %all_to_all.11 = f32[16,40,128]{2,1,0:T(8,128)S(1)} all-to-all(f32[16,40,128]{2,1,0:T(8,128)S(1)} %chain.1), channel_id=1, replica_groups=mesh['ctx'=16,'ch'=8] {'ctx'}, dimensions={0} | all-to-all | bytes 655360 | tf_op jit(solution)/shard_map/all_to_all | solution.py:562
  39.9 1.4 %collective-permute-start = (f32[8,128]{1,0:T(8,128)S(1)}, f32[8,128]{1,0:T(8,128)S(1)}, u32[]{:S(2)}, u32[]{:S(2)}) collective-permute-start(f32[8,128]{1,0:T(8,128)S(1)} %norm.1), channel_id=1, source_target_pairs={{0,2},{1,3},{2,0},{3,1},{4,6},{5,7},{6,4},{7,5},{8,10},{9,11},{10,... | collective-permute-start | bytes 12296 | tf_op jit(solution)/shard_map/ppermute | solution.py:545
  41.3 3.1 %adjoint.1.ig_buf = bf16[8,512,128]{2,1,0:T(8,128)(2,1)S(1)} custom-call(f32[8,64,8,128]{3,2,1,0:T(8,128)S(1)} %get-tuple-element.32.sq_ref, f32[8,16,8,128]{3,2,1,0:T(8,128)S(1)} %get-tuple-element.33.lam_ref, f32[8,16,8,128]{3,2,1,0:T(8,128)S(1)} %get-tuple-element.34.mu_ref, f32[8,8,8,128]{3,2,1,0:T(8,128)S(1)} %get-tuple-element.35.near_ref, ...), custom_call_target="tpu_custom_call" | custom-call | flops 335544320 | bytes 8388608 | tf_op jit(solution)/shard_map/adjoint/pallas_call | solution.py:503
  44.4 0.0 collective-permute-done
  44.4 2.7 %collective-permute-start.1 = (f32[8,128]{1,0:T(8,128)S(1)}, f32[8,128]{1,0:T(8,128)S(1)}, u32[]{:S(2)}, u32[]{:S(2)}) collective-permute-start(f32[8,128]{1,0:T(8,128)S(1)} %add.6), channel_id=1, source_target_pairs={{0,4},{1,5},{2,6},{3,7},{4,0},{5,1},{6,2},{7,3},{8,12},{9,13},{10,... | collective-permute-start | bytes 12296 | tf_op jit(solution)/shard_map/ppermute | solution.py:545
  47.1 3.5 %gate.1 = (bf16[512,1024]{1,0:T(8,128)(2,1)}, bf16[512,1024]{1,0:T(8,128)(2,1)}, bf16[2,512,128]{2,1,0:T(8,128)(2,1)S(1)}) custom-call(bf16[8,512,128]{2,1,0:T(8,128)(2,1)S(1)} %adjoint.1.ig_buf, bf16[8,512,128]{2,1,0:T(8,128)(2,1)S(1)} %get-tuple-element.39.g_buf, f32[8,64,8,128]{3,2,1,0:T(8,128)S(1)} %get-tuple-element.40.xq_ref, ...), custom_call_target="tpu_custom_call" | custom-call | flops 335544320 | bytes 8388608 | tf_op jit(solution)/shard_map/gate/pallas_call | solution.py:522
  50.6 0.0 collective-permute-done.1
  50.6 3.9 %collective-permute-start.2 = (f32[8,128]{1,0:T(8,128)S(1)}, f32[8,128]{1,0:T(8,128)S(1)}, u32[]{:S(2)}, u32[]{:S(2)}) collective-permute-start(f32[8,128]{1,0:T(8,128)S(1)} %add.7.own_ref), channel_id=1, source_target_pairs={{0,1},{1,0},{2,3},{3,2},{4,5},{5,4},{6,7},{7,6},{8,9},{9,8},{10,11... | collective-permute-start | bytes 12296 | tf_op jit(solution)/shard_map/ppermute | solution.py:545
  54.6 0.8 %collective-permute-done.2.other_ref = f32[8,128]{1,0:T(8,128)S(1)} collective-permute-done((f32[8,128]{1,0:T(8,128)S(1)}, f32[8,128]{1,0:T(8,128)S(1)}, u32[]{:S(2)}, u32[]{:S(2)}) %collective-permute-start.2) | collective-permute-done | bytes 4128 | tf_op jit(solution)/shard_map/ppermute | solution.py:545
  55.4 0.8 %scale.1 = (f32[16,1024]{1,0:T(8,128)}, f32[16,1024]{1,0:T(8,128)}, f32[8,128]{1,0:T(8,128)}, bf16[512,1024]{1,0:T(8,128)(2,1)}) custom-call(f32[8,128]{1,0:T(8,128)S(1)} %add.7.own_ref, f32[8,128]{1,0:T(8,128)S(1)} %collective-permute-done.2.other_ref, f32[640,128]{1,0:T(8,128)S(1)} %bitcast.7, ...), custom_call_target="tpu_custom_call", output_to_operand_aliasing={{3}: (5, {})} | custom-call | tf_op jit(solution)/shard_map/scale/pallas_call | solution.py:579
  (3 shorter events, 0.1 us)
Async XLA Ops:
  39.9 4.5 %collective-permute-start = (f32[8,128]{1,0:T(8,128)S(1)}, f32[8,128]{1,0:T(8,128)S(1)}, u32[]{:S(2)}, u32[]{:S(2)}) collective-permute-start(f32[8,128]{1,0:T(8,128)S(1)} %norm.1), channel_id=1, source_target_pairs={{0,2},{1,3},{2,0},{3,1},{4,6},{5,7},{6,4},{7,5},{8,10},{9,11},{10,... | collective-permute-start | bytes 12296 | tf_op jit(solution)/shard_map/ppermute | solution.py:545
  44.4 6.2 %collective-permute-start.1 = (f32[8,128]{1,0:T(8,128)S(1)}, f32[8,128]{1,0:T(8,128)S(1)}, u32[]{:S(2)}, u32[]{:S(2)}) collective-permute-start(f32[8,128]{1,0:T(8,128)S(1)} %add.6), channel_id=1, source_target_pairs={{0,4},{1,5},{2,6},{3,7},{4,0},{5,1},{6,2},{7,3},{8,12},{9,13},{10,... | collective-permute-start | bytes 12296 | tf_op jit(solution)/shard_map/ppermute | solution.py:545
  50.6 4.8 %collective-permute-start.2 = (f32[8,128]{1,0:T(8,128)S(1)}, f32[8,128]{1,0:T(8,128)S(1)}, u32[]{:S(2)}, u32[]{:S(2)}) collective-permute-start(f32[8,128]{1,0:T(8,128)S(1)} %add.7.own_ref), channel_id=1, source_target_pairs={{0,1},{1,0},{2,3},{3,2},{4,5},{5,4},{6,7},{7,6},{8,9},{9,8},{10,11... | collective-permute-start | bytes 12296 | tf_op jit(solution)/shard_map/ppermute | solution.py:545

commit v4 on v3

--- a/solution.py
+++ b/solution.py
@@ -399,7 +399,7 @@
 
 
 def scale_kernel(
-    own_ref, other_ref, back_ref, rows_ref, late_ref, part_hbm,
+    own_ref, first_ref, second_ref, third_ref, back_ref, rows_ref, late_ref, part_hbm,
     rg_hbm, lg_hbm, sg_hbm, gg_hbm,
     rg_buf, lg_buf, sg_buf, late_sem, sem,
 ):
@@ -412,7 +412,8 @@
     ]
     for copy in copies:
         copy.start()
-    sums = jnp.sum(own_ref[...] + other_ref[...], axis=1, keepdims=True)
+    total = (own_ref[...] + first_ref[...]) + (second_ref[...] + third_ref[...])
+    sums = jnp.sum(total, axis=1, keepdims=True)
 
     def factor(n, ceiling):
         return jnp.minimum(1.0, ceiling / jnp.sqrt(sums[n : n + 1, :] + 1e-06))
@@ -567,18 +568,14 @@
         compiler_params=params(),
         name="norm",
     )(back, rows)
-    first = swapped(squares, 2)
+    squares = squares + swapped(squares, 1)
+    others = [swapped(squares, bit) for bit in (2, 4, 6)]
     ig = back_call(tokens, sq, lam, mu, near, rows, al, as_, back)
-    first, ig = lax.optimization_barrier((first, ig))
-    squares = squares + first
-    second = swapped(squares, 4)
     input_grad, gate_grad, late = gate_call(ig, g, xq, lam, mu, near, rows, hl, hs, back)
-    second, late = lax.optimization_barrier((second, late))
-    squares = squares + second
-    other = swapped(squares, 1)
+    *others, late = lax.optimization_barrier((*others, late))
     res_out, log_out, skip_out, gate_grad = pl.pallas_call(
         scale_kernel,
-        in_specs=[VMEM] * 5 + [HBM],
+        in_specs=[VMEM] * 7 + [HBM],
         out_specs=[HBM] * 4,
         out_shape=[
             shape(MODES, chan), shape(MODES, chan), shape(groups, LANES),
@@ -591,10 +588,10 @@
             pltpu.SemaphoreType.DMA((LATE,)),
             pltpu.SemaphoreType.DMA((3,)),
         ],
-        input_output_aliases={5: 3},
+        input_output_aliases={7: 3},
         compiler_params=params(),
         name="scale",
-    )(squares, other, back, rows, late, gate_grad)
+    )(squares, *others, back, rows, late, gate_grad)
     return input_grad, gate_grad, res_out, log_out, skip_out.reshape(chan)
 
 

time: 56.4 us -> 54.4 us (0.965)
  starting transfers between devices: 8.01 us -> 6.86 us
  waiting for transfers between devices: 0.83 us -> 0.01 us
    ppermute x3 -> x4, starting transfers between devices: 8.01 us -> 6.86 us  [swapped(): return lax.ppermute(value, 'ch', [(i, i ^ bit) for i in range(peers)])]
    ppermute x3 -> x4, waiting for transfers between devices: 0.83 us -> 0.01 us  [swapped(): return lax.ppermute(value, 'ch', [(i, i ^ bit) for i in range(peers)])]
  transfers between devices with their start and end apart: 3 -> 4, of which waited for: 1 -> 0; matrix products, arithmetic and copies ran while one was open for 0% -> 0% of each run, Pallas kernels for 12% -> 12%
where the time goes in v4:
time: 54.4 us; the launch traced here: 54.2 us
  blocking collectives  28 us (51%)
  Pallas kernels  18.6 us (34%)
  starting transfers between devices  6.86 us (13%)
  between operations  0.7 us (1%)
    all_to_all x1, blocking collectives, on_device(): got = lax.all_to_all(pay.reshape(spans, SENT, LANES), 'ctx', 0, 0)  16.5 us
    all_to_all x1, blocking collectives, on_device(): back = lax.all_to_all(back, 'ctx', 0, 0).reshape(MODES * BACK, LANES)  11.6 us
    pallas_call x1, Pallas kernels, span_call(): pl.pallas_call(span_kernel, in_specs=[HBM] * 6, out_specs=[VMEM] * 13, ou...  11.1 us
    ppermute x4, starting transfers between devices, swapped(): return lax.ppermute(value, 'ch', [(i, i ^ bit) for i in range(peers)])  6.86 us
    pallas_call x1, Pallas kernels, gate_call(): pl.pallas_call(gate_kernel, in_specs=[VMEM] * 10, out_specs=[HBM, HBM, VM...  3.47 us
    pallas_call x1, Pallas kernels, back_call(): pl.pallas_call(back_kernel, in_specs=[VMEM] * 8, out_specs=VMEM, out_shap...  3.12 us
  transfers between devices with their start and end apart: 4, of which 0 were waited for; matrix products, arithmetic and copies ran while one was open for 0% of the time, Pallas kernels for 12%

profile of v4, /device:TPU:1, one launch (start us, length us, event | category | flops | bytes accessed | tf_op | source)
XLA Modules:
  0.0 54.2 jit_solution(8663041277790640567)
XLA Ops:
  0.6 11.1 %span.1 = (f32[8,8,16,8,128]{4,3,2,1,0:T(8,128)S(1)}, f32[8,8,16,8,128]{4,3,2,1,0:T(8,128)S(1)}, f32[8,8,16,128]{3,2,1,0:T(8,128)S(1)}, f32[8,8,16,128]{3,2,1,0:...) custom-call(bf16[512,1024]{1,0:T(8,128)(2,1)} %x_hbm.1, ...), custom_call_target="tpu_custom_call" | custom-call | tf_op jit(solution)/shard_map/span/pallas_call | solution.py:466
  11.7 16.5 %all_to_all.10.got_ref = f32[16,48,128]{2,1,0:T(8,128)S(1)} all-to-all(f32[16,48,128]{2,1,0:T(8,128)S(1)} %bitcast.8), channel_id=1, replica_groups=mesh['ctx'=16,'ch'=8] {'ctx'}, dimensions={0} | all-to-all | bytes 786432 | tf_op jit(solution)/shard_map/all_to_all | solution.py:556
  28.2 0.1 chain.1
  28.3 11.6 %all_to_all.11 = f32[16,40,128]{2,1,0:T(8,128)S(1)} all-to-all(f32[16,40,128]{2,1,0:T(8,128)S(1)} %chain.1), channel_id=1, replica_groups=mesh['ctx'=16,'ch'=8] {'ctx'}, dimensions={0} | all-to-all | bytes 655360 | tf_op jit(solution)/shard_map/all_to_all | solution.py:563
  39.9 3.4 %collective-permute-start = (f32[8,128]{1,0:T(8,128)S(1)}, f32[8,128]{1,0:T(8,128)S(1)}, u32[]{:S(2)}, u32[]{:S(2)}) collective-permute-start(f32[8,128]{1,0:T(8,128)S(1)} %norm.1), channel_id=1, source_target_pairs={{0,1},{1,0},{2,3},{3,2},{4,5},{5,4},{6,7},{7,6},{8,9},{9,8},{10,11... | collective-permute-start | bytes 12296 | tf_op jit(solution)/shard_map/ppermute | solution.py:546
  43.3 3.1 %adjoint.1.ig_buf = bf16[8,512,128]{2,1,0:T(8,128)(2,1)S(1)} custom-call(f32[8,64,8,128]{3,2,1,0:T(8,128)S(1)} %get-tuple-element.29.sq_ref, f32[8,16,8,128]{3,2,1,0:T(8,128)S(1)} %get-tuple-element.30.lam_ref, f32[8,16,8,128]{3,2,1,0:T(8,128)S(1)} %get-tuple-element.31.mu_ref, f32[8,8,8,128]{3,2,1,0:T(8,128)S(1)} %get-tuple-element.32.near_ref, ...), custom_call_target="tpu_custom_call" | custom-call | flops 335544320 | bytes 8388608 | tf_op jit(solution)/shard_map/adjoint/pallas_call | solution.py:504
  46.4 0.0 collective-permute-done
  46.4 2.8 %collective-permute-start.3 = (f32[8,128]{1,0:T(8,128)S(1)}, f32[8,128]{1,0:T(8,128)S(1)}, u32[]{:S(2)}, u32[]{:S(2)}) collective-permute-start(f32[8,128]{1,0:T(8,128)S(1)} %add.3.own_ref), channel_id=1, source_target_pairs={{0,6},{1,7},{2,4},{3,5},{4,2},{5,3},{6,0},{7,1},{8,14},{9,15},{10,... | collective-permute-start | bytes 12296 | tf_op jit(solution)/shard_map/ppermute | solution.py:546
  49.2 0.3 collective-permute-start.2
  49.6 0.3 collective-permute-start.1
  49.9 3.5 %gate.1 = (bf16[512,1024]{1,0:T(8,128)(2,1)}, bf16[512,1024]{1,0:T(8,128)(2,1)}, bf16[2,512,128]{2,1,0:T(8,128)(2,1)S(1)}) custom-call(bf16[8,512,128]{2,1,0:T(8,128)(2,1)S(1)} %adjoint.1.ig_buf, bf16[8,512,128]{2,1,0:T(8,128)(2,1)S(1)} %get-tuple-element.38.g_buf, f32[8,64,8,128]{3,2,1,0:T(8,128)S(1)} %get-tuple-element.39.xq_ref, ...), custom_call_target="tpu_custom_call" | custom-call | flops 335544320 | bytes 8388608 | tf_op jit(solution)/shard_map/gate/pallas_call | solution.py:523
  53.4 0.0 collective-permute-done.3.third_ref
  53.4 0.0 collective-permute-done.2.second_ref
  53.4 0.0 collective-permute-done.1.first_ref
  53.4 0.8 %scale.1 = (f32[16,1024]{1,0:T(8,128)}, f32[16,1024]{1,0:T(8,128)}, f32[8,128]{1,0:T(8,128)}, bf16[512,1024]{1,0:T(8,128)(2,1)}) custom-call(f32[8,128]{1,0:T(8,128)S(1)} %add.3.own_ref, f32[8,128]{1,0:T(8,128)S(1)} %collective-permute-done.1.first_ref, f32[8,128]{1,0:T(8,128)S(1)} %collective-permute-done.2.second_ref, ...), custom_call_target="tpu_custom_call", output_to_operand_aliasing={{3}: (7, {})} | custom-call | tf_op jit(solution)/shard_map/scale/pallas_call | solution.py:576
  (2 shorter events, 0.1 us)
Async XLA Ops:
  39.9 6.5 %collective-permute-start = (f32[8,128]{1,0:T(8,128)S(1)}, f32[8,128]{1,0:T(8,128)S(1)}, u32[]{:S(2)}, u32[]{:S(2)}) collective-permute-start(f32[8,128]{1,0:T(8,128)S(1)} %norm.1), channel_id=1, source_target_pairs={{0,1},{1,0},{2,3},{3,2},{4,5},{5,4},{6,7},{7,6},{8,9},{9,8},{10,11... | collective-permute-start | bytes 12296 | tf_op jit(solution)/shard_map/ppermute | solution.py:546
  46.4 7.0 %collective-permute-start.3 = (f32[8,128]{1,0:T(8,128)S(1)}, f32[8,128]{1,0:T(8,128)S(1)}, u32[]{:S(2)}, u32[]{:S(2)}) collective-permute-start(f32[8,128]{1,0:T(8,128)S(1)} %add.3.own_ref), channel_id=1, source_target_pairs={{0,6},{1,7},{2,4},{3,5},{4,2},{5,3},{6,0},{7,1},{8,14},{9,15},{10,... | collective-permute-start | bytes 12296 | tf_op jit(solution)/shard_map/ppermute | solution.py:546
  49.2 4.2 %collective-permute-start.2 = (f32[8,128]{1,0:T(8,128)S(1)}, f32[8,128]{1,0:T(8,128)S(1)}, u32[]{:S(2)}, u32[]{:S(2)}) collective-permute-start(f32[8,128]{1,0:T(8,128)S(1)} %add.3.own_ref), channel_id=1, source_target_pairs={{0,4},{1,5},{2,6},{3,7},{4,0},{5,1},{6,2},{7,3},{8,12},{9,13},{10,... | collective-permute-start | bytes 12296 | tf_op jit(solution)/shard_map/ppermute | solution.py:546
  49.6 3.8 %collective-permute-start.1 = (f32[8,128]{1,0:T(8,128)S(1)}, f32[8,128]{1,0:T(8,128)S(1)}, u32[]{:S(2)}, u32[]{:S(2)}) collective-permute-start(f32[8,128]{1,0:T(8,128)S(1)} %add.3.own_ref), channel_id=1, source_target_pairs={{0,2},{1,3},{2,0},{3,1},{4,6},{5,7},{6,4},{7,5},{8,10},{9,11},{10,... | collective-permute-start | bytes 12296 | tf_op jit(solution)/shard_map/ppermute | solution.py:546

commit v5 on v4

--- a/solution.py
+++ b/solution.py
@@ -14,6 +14,7 @@
 SEGS = 8
 SUB = 8
 F32 = jnp.float32
+FIRST = 6
 LATE = 2
 AHEAD = 2
 END_PITCH = 9
@@ -274,17 +275,41 @@
             state = state * big
 
 
-def far(total, indices, local_ref, group, k, lam_ref, mu_ref, run):
+def far(total, indices, local_ref, group, k, step, chunks, lam_ref, mu_ref, run):
     for m in range(MODES):
         here = pl.ds(m * SEGS, SEGS)
-        step = lam_ref[group, m]
+        decay = lam_ref[group, m]
         state = run[here, :]
-        c = local_ref[group, k, m] + state
-        run[here, :] = state * mu_ref[group, m]
+        c = state if step == 0 else local_ref[group, k, m] + state
+        if step < chunks - 1:
+            run[here, :] = state * mu_ref[group, m]
         for i in indices:
             total[i] = total[i] + c
             if i != indices[-1]:
-                c = c * step
+                c = c * decay
+
+
+def adjoint_block(
+    group, seg_len, sq_ref, lam_ref, mu_ref, near_ref, rows_ref, al_ref, as_ref, back_ref,
+    natural, run,
+):
+    chunks = seg_len // SUB
+    entering(group, 8, back_ref, rows_ref, as_ref, run, True)
+    for step in range(chunks):
+        k = chunks - 1 - step
+        near = [near_ref[group, d] for d in range(SUB)]
+        ss = [sq_ref[group, k * SUB + j] for j in range(SUB)]
+        total = []
+        for j in range(SUB):
+            value = near[0] * ss[j]
+            for d in range(1, SUB - j):
+                value = value + near[d] * ss[j + d]
+            total.append(value)
+        order = list(reversed(range(SUB)))
+        far(total, order, al_ref, group, k, step, chunks, lam_ref, mu_ref, run)
+        for j in range(SUB):
+            natural[pl.ds(k * SUB + j, SEGS, stride=PITCH), :] = total[j]
+    return natural_order(natural, seg_len).astype(jnp.bfloat16)
 
 
 def back_kernel(
@@ -292,51 +317,51 @@
     ig_ref,
     natural, run,
 ):
-    groups, tokens, _ = ig_ref.shape
-    seg_len = tokens // SEGS
-    chunks = seg_len // SUB
+    first, tokens, _ = ig_ref.shape
 
     def group_step(group, carry):
-        entering(group, 8, back_ref, rows_ref, as_ref, run, True)
-
-        def chunk_step(step, carry):
-            k = chunks - 1 - step
-            near = [near_ref[group, d] for d in range(SUB)]
-            ss = [sq_ref[group, k * SUB + j] for j in range(SUB)]
-            total = []
-            for j in range(SUB):
-                value = near[0] * ss[j]
-                for d in range(1, SUB - j):
-                    value = value + near[d] * ss[j + d]
-                total.append(value)
-            far(total, list(reversed(range(SUB))), al_ref, group, k, lam_ref, mu_ref, run)
-            for j in range(SUB):
-                natural[pl.ds(k * SUB + j, SEGS, stride=PITCH), :] = total[j]
-            return carry
-
-        lax.fori_loop(0, chunks, chunk_step, 0, unroll=8)
-        ig_ref[group] = natural_order(natural, seg_len).astype(jnp.bfloat16)
+        ig_ref[group] = adjoint_block(
+            group, tokens // SEGS, sq_ref, lam_ref, mu_ref, near_ref, rows_ref, al_ref, as_ref,
+            back_ref, natural, run,
+        )
         return carry
 
-    lax.fori_loop(0, groups, group_step, 0)
+    lax.fori_loop(0, first, group_step, 0)
 
 
 def gate_kernel(
-    ig_buf, g_buf, xq_ref, lam_ref, mu_ref, near_ref, rows_ref, hl_ref, hs_ref, back_ref,
+    ig_buf, g_buf, xq_ref, sq_ref, lam_ref, mu_ref, near_ref, rows_ref,
+    hl_ref, hs_ref, al_ref, as_ref, back_ref,
     ig_hbm, gg_hbm, late_ref,
-    natural, run, buf, ig_sem, sem,
+    natural, run, ig_late, buf, ig_sem, sem,
 ):
     groups, tokens, _ = g_buf.shape
+    first = ig_buf.shape[0]
     early = groups - LATE
     seg_len = tokens // SEGS
     chunks = seg_len // SUB
-    for group in range(groups):
+
+    def late_copy(group):
+        return pltpu.make_async_copy(
+            ig_late.at[group - first], ig_hbm.at[:, columns(group)], ig_sem.at[group]
+        )
+
+    for group in range(first):
         put(ig_hbm, ig_buf, ig_sem, group).start()
+
+    def adjoint_step(group, carry):
+        ig_late[group - first] = adjoint_block(
+            group, seg_len, sq_ref, lam_ref, mu_ref, near_ref, rows_ref, al_ref, as_ref,
+            back_ref, natural, run,
+        )
+        late_copy(group).start()
+        return carry
+
+    lax.fori_loop(first, groups, adjoint_step, 0)
 
     def group_step(group, carry):
         entering(group, 0, back_ref, rows_ref, hs_ref, run, False)
-
-        def chunk_step(k, carry):
+        for k in range(chunks):
             near = [near_ref[group, d] for d in range(SUB)]
             xs = [xq_ref[group, k * SUB + j] for j in range(SUB)]
             total = []
@@ -345,12 +370,9 @@
                 for d in range(1, i + 1):
                     value = value + near[d] * xs[i - d]
                 total.append(value)
-            far(total, list(range(SUB)), hl_ref, group, k, lam_ref, mu_ref, run)
+            far(total, list(range(SUB)), hl_ref, group, k, k, chunks, lam_ref, mu_ref, run)
             for i in range(SUB):
                 natural[pl.ds(k * SUB + i, SEGS, stride=PITCH), :] = total[i]
-            return carry
-
-        lax.fori_loop(0, chunks, chunk_step, 0, unroll=8)
         mixed = natural_order(natural, seg_len)
         gated = (g_buf[group].astype(F32) * mixed).astype(jnp.bfloat16)
 
@@ -367,7 +389,10 @@
 
     lax.fori_loop(0, groups, group_step, 0)
     for group in range(groups):
-        put(ig_hbm, ig_buf, ig_sem, group).wait()
+        if group < first:
+            put(ig_hbm, ig_buf, ig_sem, group).wait()
+        else:
+            late_copy(group).wait()
         if group < early:
             put(gg_hbm, buf, sem, group).wait()
 
@@ -505,7 +530,7 @@
         back_kernel,
         in_specs=[VMEM] * 8,
         out_specs=VMEM,
-        out_shape=jax.ShapeDtypeStruct((groups, tokens, LANES), jnp.bfloat16),
+        out_shape=jax.ShapeDtypeStruct((min(FIRST, groups), tokens, LANES), jnp.bfloat16),
         scratch_shapes=[
             pltpu.VMEM((SEGS * PITCH, LANES), F32),
             pltpu.VMEM((MODES * SEGS, LANES), F32),
@@ -516,13 +541,13 @@
     )(sq, lam, mu, near, rows, al, as_, back)
 
 
-def gate_call(ig, g, xq, lam, mu, near, rows, hl, hs, back):
+def gate_call(ig, g, xq, sq, lam, mu, near, rows, hl, hs, al, as_, back):
     groups, tokens, _ = g.shape
     chan = groups * LANES
     sems = pltpu.SemaphoreType.DMA((groups,))
     return pl.pallas_call(
         gate_kernel,
-        in_specs=[VMEM] * 10,
+        in_specs=[VMEM] * 13,
         out_specs=[HBM, HBM, VMEM],
         out_shape=[
             jax.ShapeDtypeStruct((tokens, chan), jnp.bfloat16),
@@ -532,13 +557,14 @@
         scratch_shapes=[
             pltpu.VMEM((SEGS * PITCH, LANES), F32),
             pltpu.VMEM((MODES * SEGS, LANES), F32),
+            pltpu.VMEM((groups - ig.shape[0], tokens, LANES), jnp.bfloat16),
             pltpu.VMEM((groups - LATE, tokens, LANES), jnp.bfloat16),
             sems, sems,
         ],
         compiler_params=params(),
         cost_estimate=work(40 * MODES * tokens * chan, 16 * tokens * chan),
         name="gate",
-    )(ig, g, xq, lam, mu, near, rows, hl, hs, back)
+    )(ig, g, xq, sq, lam, mu, near, rows, hl, hs, al, as_, back)
 
 
 def swapped(value, bit):
@@ -569,9 +595,11 @@
         name="norm",
     )(back, rows)
     squares = squares + swapped(squares, 1)
-    others = [swapped(squares, bit) for bit in (2, 4, 6)]
+    others = [swapped(squares, bit) for bit in (6, 4, 2)]
     ig = back_call(tokens, sq, lam, mu, near, rows, al, as_, back)
-    input_grad, gate_grad, late = gate_call(ig, g, xq, lam, mu, near, rows, hl, hs, back)
+    input_grad, gate_grad, late = gate_call(
+        ig, g, xq, sq, lam, mu, near, rows, hl, hs, al, as_, back
+    )
     *others, late = lax.optimization_barrier((*others, late))
     res_out, log_out, skip_out, gate_grad = pl.pallas_call(
         scale_kernel,

time: 54.4 us -> 54.3 us (level)
    pallas_call x1, Pallas kernels: 3.12 us -> 2.3 us  [back_call(): pl.pallas_call(back_kernel, in_specs=[VMEM] * 8, out_specs=VMEM, out_shap...]
    pallas_call x1, Pallas kernels: 3.47 us -> 4.2 us  [gate_call(): pl.pallas_call(gate_kernel, in_specs=[VMEM] * 13, out_specs=[HBM, HBM, VM...]
where the time goes in v5:
time: 54.3 us; the launch traced here: 54.1 us
  blocking collectives  28 us (52%)
  Pallas kernels  18.5 us (34%)
  starting transfers between devices  6.86 us (13%)
  between operations  0.7 us (1%)
    all_to_all x1, blocking collectives, on_device(): got = lax.all_to_all(pay.reshape(spans, SENT, LANES), 'ctx', 0, 0)  16.5 us
    all_to_all x1, blocking collectives, on_device(): back = lax.all_to_all(back, 'ctx', 0, 0).reshape(MODES * BACK, LANES)  11.6 us
    pallas_call x1, Pallas kernels, span_call(): pl.pallas_call(span_kernel, in_specs=[HBM] * 6, out_specs=[VMEM] * 13, ou...  11.1 us
    ppermute x4, starting transfers between devices, swapped(): return lax.ppermute(value, 'ch', [(i, i ^ bit) for i in range(peers)])  6.86 us
    pallas_call x1, Pallas kernels, gate_call(): pl.pallas_call(gate_kernel, in_specs=[VMEM] * 13, out_specs=[HBM, HBM, VM...  4.2 us
    pallas_call x1, Pallas kernels, back_call(): pl.pallas_call(back_kernel, in_specs=[VMEM] * 8, out_specs=VMEM, out_shap...  2.3 us
  transfers between devices with their start and end apart: 4, of which 0 were waited for; matrix products, arithmetic and copies ran while one was open for 0% of the time, Pallas kernels for 12%

profile of v5, /device:TPU:1, one launch (start us, length us, event | category | flops | bytes accessed | tf_op | source)
XLA Modules:
  0.0 54.1 jit_solution(14507486248108674575)
XLA Ops:
  0.6 11.1 %span.1 = (f32[8,8,16,8,128]{4,3,2,1,0:T(8,128)S(1)}, f32[8,8,16,8,128]{4,3,2,1,0:T(8,128)S(1)}, f32[8,8,16,128]{3,2,1,0:T(8,128)S(1)}, f32[8,8,16,128]{3,2,1,0:...) custom-call(bf16[512,1024]{1,0:T(8,128)(2,1)} %x_hbm.1, ...), custom_call_target="tpu_custom_call" | custom-call | tf_op jit(solution)/shard_map/span/pallas_call | solution.py:491
  11.7 16.5 %all_to_all.10.got_ref = f32[16,48,128]{2,1,0:T(8,128)S(1)} all-to-all(f32[16,48,128]{2,1,0:T(8,128)S(1)} %bitcast.8), channel_id=1, replica_groups=mesh['ctx'=16,'ch'=8] {'ctx'}, dimensions={0} | all-to-all | bytes 786432 | tf_op jit(solution)/shard_map/all_to_all | solution.py:582
  28.2 0.1 chain.1
  28.3 11.6 %all_to_all.11 = f32[16,40,128]{2,1,0:T(8,128)S(1)} all-to-all(f32[16,40,128]{2,1,0:T(8,128)S(1)} %chain.1), channel_id=1, replica_groups=mesh['ctx'=16,'ch'=8] {'ctx'}, dimensions={0} | all-to-all | bytes 655360 | tf_op jit(solution)/shard_map/all_to_all | solution.py:589
  39.9 3.4 %collective-permute-start = (f32[8,128]{1,0:T(8,128)S(1)}, f32[8,128]{1,0:T(8,128)S(1)}, u32[]{:S(2)}, u32[]{:S(2)}) collective-permute-start(f32[8,128]{1,0:T(8,128)S(1)} %norm.1), channel_id=1, source_target_pairs={{0,1},{1,0},{2,3},{3,2},{4,5},{5,4},{6,7},{7,6},{8,9},{9,8},{10,11... | collective-permute-start | bytes 12296 | tf_op jit(solution)/shard_map/ppermute | solution.py:572
  43.3 2.3 %adjoint.1.ig_buf = bf16[6,512,128]{2,1,0:T(8,128)(2,1)S(1)} custom-call(f32[8,64,8,128]{3,2,1,0:T(8,128)S(1)} %get-tuple-element.29.sq_ref, f32[8,16,8,128]{3,2,1,0:T(8,128)S(1)} %get-tuple-element.30.lam_ref, f32[8,16,8,128]{3,2,1,0:T(8,128)S(1)} %get-tuple-element.31.mu_ref, f32[8,8,8,128]{3,2,1,0:T(8,128)S(1)} %get-tuple-element.32.near_ref, ...), custom_call_target="tpu_custom_call" | custom-call | flops 335544320 | bytes 8388608 | tf_op jit(solution)/shard_map/adjoint/pallas_call | solution.py:529
  45.6 0.0 collective-permute-done
  45.6 2.8 %collective-permute-start.1 = (f32[8,128]{1,0:T(8,128)S(1)}, f32[8,128]{1,0:T(8,128)S(1)}, u32[]{:S(2)}, u32[]{:S(2)}) collective-permute-start(f32[8,128]{1,0:T(8,128)S(1)} %add.3.own_ref), channel_id=1, source_target_pairs={{0,6},{1,7},{2,4},{3,5},{4,2},{5,3},{6,0},{7,1},{8,14},{9,15},{10,... | collective-permute-start | bytes 12296 | tf_op jit(solution)/shard_map/ppermute | solution.py:572
  48.4 0.3 collective-permute-start.2
  48.8 0.3 collective-permute-start.3
  49.1 4.2 %gate.1 = (bf16[512,1024]{1,0:T(8,128)(2,1)}, bf16[512,1024]{1,0:T(8,128)(2,1)}, bf16[2,512,128]{2,1,0:T(8,128)(2,1)S(1)}) custom-call(bf16[6,512,128]{2,1,0:T(8,128)(2,1)S(1)} %adjoint.1.ig_buf, bf16[8,512,128]{2,1,0:T(8,128)(2,1)S(1)} %get-tuple-element.38.g_buf, f32[8,64,8,128]{3,2,1,0:T(8,128)S(1)} %get-tuple-element.39.xq_ref, ...), custom_call_target="tpu_custom_call" | custom-call | flops 335544320 | bytes 8388608 | tf_op jit(solution)/shard_map/gate/pallas_call | solution.py:548
  53.3 0.0 collective-permute-done.1.first_ref
  53.3 0.0 collective-permute-done.2.second_ref
  53.3 0.0 collective-permute-done.3.third_ref
  53.3 0.8 %scale.1 = (f32[16,1024]{1,0:T(8,128)}, f32[16,1024]{1,0:T(8,128)}, f32[8,128]{1,0:T(8,128)}, bf16[512,1024]{1,0:T(8,128)(2,1)}) custom-call(f32[8,128]{1,0:T(8,128)S(1)} %add.3.own_ref, f32[8,128]{1,0:T(8,128)S(1)} %collective-permute-done.1.first_ref, f32[8,128]{1,0:T(8,128)S(1)} %collective-permute-done.2.second_ref, ...), custom_call_target="tpu_custom_call", output_to_operand_aliasing={{3}: (7, {})} | custom-call | tf_op jit(solution)/shard_map/scale/pallas_call | solution.py:604
  (2 shorter events, 0.1 us)
Async XLA Ops:
  39.9 5.7 %collective-permute-start = (f32[8,128]{1,0:T(8,128)S(1)}, f32[8,128]{1,0:T(8,128)S(1)}, u32[]{:S(2)}, u32[]{:S(2)}) collective-permute-start(f32[8,128]{1,0:T(8,128)S(1)} %norm.1), channel_id=1, source_target_pairs={{0,1},{1,0},{2,3},{3,2},{4,5},{5,4},{6,7},{7,6},{8,9},{9,8},{10,11... | collective-permute-start | bytes 12296 | tf_op jit(solution)/shard_map/ppermute | solution.py:572
  45.6 7.7 %collective-permute-start.1 = (f32[8,128]{1,0:T(8,128)S(1)}, f32[8,128]{1,0:T(8,128)S(1)}, u32[]{:S(2)}, u32[]{:S(2)}) collective-permute-start(f32[8,128]{1,0:T(8,128)S(1)} %add.3.own_ref), channel_id=1, source_target_pairs={{0,6},{1,7},{2,4},{3,5},{4,2},{5,3},{6,0},{7,1},{8,14},{9,15},{10,... | collective-permute-start | bytes 12296 | tf_op jit(solution)/shard_map/ppermute | solution.py:572
  48.4 4.9 %collective-permute-start.2 = (f32[8,128]{1,0:T(8,128)S(1)}, f32[8,128]{1,0:T(8,128)S(1)}, u32[]{:S(2)}, u32[]{:S(2)}) collective-permute-start(f32[8,128]{1,0:T(8,128)S(1)} %add.3.own_ref), channel_id=1, source_target_pairs={{0,4},{1,5},{2,6},{3,7},{4,0},{5,1},{6,2},{7,3},{8,12},{9,13},{10,... | collective-permute-start | bytes 12296 | tf_op jit(solution)/shard_map/ppermute | solution.py:572
  48.8 4.6 %collective-permute-start.3 = (f32[8,128]{1,0:T(8,128)S(1)}, f32[8,128]{1,0:T(8,128)S(1)}, u32[]{:S(2)}, u32[]{:S(2)}) collective-permute-start(f32[8,128]{1,0:T(8,128)S(1)} %add.3.own_ref), channel_id=1, source_target_pairs={{0,2},{1,3},{2,0},{3,1},{4,6},{5,7},{6,4},{7,5},{8,10},{9,11},{10,... | collective-permute-start | bytes 12296 | tf_op jit(solution)/shard_map/ppermute | solution.py:572

commit v6 on v5

--- a/solution.py
+++ b/solution.py
@@ -15,7 +15,7 @@
 SUB = 8
 F32 = jnp.float32
 FIRST = 6
-LATE = 2
+LATE = 3
 AHEAD = 2
 END_PITCH = 9
 SENT = 48

time: 54.3 us -> 54.4 us (level)
  no operation moved by 1% of the time
where the time goes in v6:
time: 54.4 us; the launch traced here: 54.2 us
  blocking collectives  28 us (51%)
  Pallas kernels  18.6 us (34%)
  starting transfers between devices  6.86 us (13%)
  between operations  0.7 us (1%)
    all_to_all x1, blocking collectives, on_device(): got = lax.all_to_all(pay.reshape(spans, SENT, LANES), 'ctx', 0, 0)  16.5 us
    all_to_all x1, blocking collectives, on_device(): back = lax.all_to_all(back, 'ctx', 0, 0).reshape(MODES * BACK, LANES)  11.6 us
    pallas_call x1, Pallas kernels, span_call(): pl.pallas_call(span_kernel, in_specs=[HBM] * 6, out_specs=[VMEM] * 13, ou...  11.1 us
    ppermute x4, starting transfers between devices, swapped(): return lax.ppermute(value, 'ch', [(i, i ^ bit) for i in range(peers)])  6.86 us
    pallas_call x1, Pallas kernels, gate_call(): pl.pallas_call(gate_kernel, in_specs=[VMEM] * 13, out_specs=[HBM, HBM, VM...  4.2 us
    pallas_call x1, Pallas kernels, back_call(): pl.pallas_call(back_kernel, in_specs=[VMEM] * 8, out_specs=VMEM, out_shap...  2.3 us
  transfers between devices with their start and end apart: 4, of which 0 were waited for; matrix products, arithmetic and copies ran while one was open for 0% of the time, Pallas kernels for 12%

profile of v6, /device:TPU:1, one launch (start us, length us, event | category | flops | bytes accessed | tf_op | source)
XLA Modules:
  0.0 54.2 jit_solution(6154032835549121963)
XLA Ops:
  0.6 11.1 %span.1 = (f32[8,8,16,8,128]{4,3,2,1,0:T(8,128)S(1)}, f32[8,8,16,8,128]{4,3,2,1,0:T(8,128)S(1)}, f32[8,8,16,128]{3,2,1,0:T(8,128)S(1)}, f32[8,8,16,128]{3,2,1,0:...) custom-call(bf16[512,1024]{1,0:T(8,128)(2,1)} %x_hbm.1, ...), custom_call_target="tpu_custom_call" | custom-call | tf_op jit(solution)/shard_map/span/pallas_call | solution.py:491
  11.7 16.5 %all_to_all.10.got_ref = f32[16,48,128]{2,1,0:T(8,128)S(1)} all-to-all(f32[16,48,128]{2,1,0:T(8,128)S(1)} %bitcast.8), channel_id=1, replica_groups=mesh['ctx'=16,'ch'=8] {'ctx'}, dimensions={0} | all-to-all | bytes 786432 | tf_op jit(solution)/shard_map/all_to_all | solution.py:582
  28.2 0.1 chain.1
  28.3 11.6 %all_to_all.11 = f32[16,40,128]{2,1,0:T(8,128)S(1)} all-to-all(f32[16,40,128]{2,1,0:T(8,128)S(1)} %chain.1), channel_id=1, replica_groups=mesh['ctx'=16,'ch'=8] {'ctx'}, dimensions={0} | all-to-all | bytes 655360 | tf_op jit(solution)/shard_map/all_to_all | solution.py:589
  39.9 3.4 %collective-permute-start = (f32[8,128]{1,0:T(8,128)S(1)}, f32[8,128]{1,0:T(8,128)S(1)}, u32[]{:S(2)}, u32[]{:S(2)}) collective-permute-start(f32[8,128]{1,0:T(8,128)S(1)} %norm.1), channel_id=1, source_target_pairs={{0,1},{1,0},{2,3},{3,2},{4,5},{5,4},{6,7},{7,6},{8,9},{9,8},{10,11... | collective-permute-start | bytes 12296 | tf_op jit(solution)/shard_map/ppermute | solution.py:572
  43.3 2.3 %adjoint.1.ig_buf = bf16[6,512,128]{2,1,0:T(8,128)(2,1)S(1)} custom-call(f32[8,64,8,128]{3,2,1,0:T(8,128)S(1)} %get-tuple-element.29.sq_ref, f32[8,16,8,128]{3,2,1,0:T(8,128)S(1)} %get-tuple-element.30.lam_ref, f32[8,16,8,128]{3,2,1,0:T(8,128)S(1)} %get-tuple-element.31.mu_ref, f32[8,8,8,128]{3,2,1,0:T(8,128)S(1)} %get-tuple-element.32.near_ref, ...), custom_call_target="tpu_custom_call" | custom-call | flops 335544320 | bytes 8388608 | tf_op jit(solution)/shard_map/adjoint/pallas_call | solution.py:529
  45.6 0.0 collective-permute-done
  45.6 2.8 %collective-permute-start.1 = (f32[8,128]{1,0:T(8,128)S(1)}, f32[8,128]{1,0:T(8,128)S(1)}, u32[]{:S(2)}, u32[]{:S(2)}) collective-permute-start(f32[8,128]{1,0:T(8,128)S(1)} %add.3.own_ref), channel_id=1, source_target_pairs={{0,6},{1,7},{2,4},{3,5},{4,2},{5,3},{6,0},{7,1},{8,14},{9,15},{10,... | collective-permute-start | bytes 12296 | tf_op jit(solution)/shard_map/ppermute | solution.py:572
  48.4 0.3 collective-permute-start.2
  48.8 0.3 collective-permute-start.3
  49.1 4.2 %gate.1 = (bf16[512,1024]{1,0:T(8,128)(2,1)}, bf16[512,1024]{1,0:T(8,128)(2,1)}, bf16[3,512,128]{2,1,0:T(8,128)(2,1)S(1)}) custom-call(bf16[6,512,128]{2,1,0:T(8,128)(2,1)S(1)} %adjoint.1.ig_buf, bf16[8,512,128]{2,1,0:T(8,128)(2,1)S(1)} %get-tuple-element.38.g_buf, f32[8,64,8,128]{3,2,1,0:T(8,128)S(1)} %get-tuple-element.39.xq_ref, ...), custom_call_target="tpu_custom_call" | custom-call | flops 335544320 | bytes 8388608 | tf_op jit(solution)/shard_map/gate/pallas_call | solution.py:548
  53.3 0.0 collective-permute-done.1.first_ref
  53.3 0.0 collective-permute-done.2.second_ref
  53.3 0.0 collective-permute-done.3.third_ref
  53.3 0.8 %scale.1 = (f32[16,1024]{1,0:T(8,128)}, f32[16,1024]{1,0:T(8,128)}, f32[8,128]{1,0:T(8,128)}, bf16[512,1024]{1,0:T(8,128)(2,1)}) custom-call(f32[8,128]{1,0:T(8,128)S(1)} %add.3.own_ref, f32[8,128]{1,0:T(8,128)S(1)} %collective-permute-done.1.first_ref, f32[8,128]{1,0:T(8,128)S(1)} %collective-permute-done.2.second_ref, ...), custom_call_target="tpu_custom_call", output_to_operand_aliasing={{3}: (7, {})} | custom-call | tf_op jit(solution)/shard_map/scale/pallas_call | solution.py:604
  (2 shorter events, 0.1 us)
Async XLA Ops:
  39.9 5.7 %collective-permute-start = (f32[8,128]{1,0:T(8,128)S(1)}, f32[8,128]{1,0:T(8,128)S(1)}, u32[]{:S(2)}, u32[]{:S(2)}) collective-permute-start(f32[8,128]{1,0:T(8,128)S(1)} %norm.1), channel_id=1, source_target_pairs={{0,1},{1,0},{2,3},{3,2},{4,5},{5,4},{6,7},{7,6},{8,9},{9,8},{10,11... | collective-permute-start | bytes 12296 | tf_op jit(solution)/shard_map/ppermute | solution.py:572
  45.6 7.7 %collective-permute-start.1 = (f32[8,128]{1,0:T(8,128)S(1)}, f32[8,128]{1,0:T(8,128)S(1)}, u32[]{:S(2)}, u32[]{:S(2)}) collective-permute-start(f32[8,128]{1,0:T(8,128)S(1)} %add.3.own_ref), channel_id=1, source_target_pairs={{0,6},{1,7},{2,4},{3,5},{4,2},{5,3},{6,0},{7,1},{8,14},{9,15},{10,... | collective-permute-start | bytes 12296 | tf_op jit(solution)/shard_map/ppermute | solution.py:572
  48.4 4.9 %collective-permute-start.2 = (f32[8,128]{1,0:T(8,128)S(1)}, f32[8,128]{1,0:T(8,128)S(1)}, u32[]{:S(2)}, u32[]{:S(2)}) collective-permute-start(f32[8,128]{1,0:T(8,128)S(1)} %add.3.own_ref), channel_id=1, source_target_pairs={{0,4},{1,5},{2,6},{3,7},{4,0},{5,1},{6,2},{7,3},{8,12},{9,13},{10,... | collective-permute-start | bytes 12296 | tf_op jit(solution)/shard_map/ppermute | solution.py:572
  48.8 4.6 %collective-permute-start.3 = (f32[8,128]{1,0:T(8,128)S(1)}, f32[8,128]{1,0:T(8,128)S(1)}, u32[]{:S(2)}, u32[]{:S(2)}) collective-permute-start(f32[8,128]{1,0:T(8,128)S(1)} %add.3.own_ref), channel_id=1, source_target_pairs={{0,2},{1,3},{2,0},{3,1},{4,6},{5,7},{6,4},{7,5},{8,10},{9,11},{10,... | collective-permute-start | bytes 12296 | tf_op jit(solution)/shard_map/ppermute | solution.py:572
